TPU v7x, 32 devices: a whole 2x2x4 slice. The times are simulated.
32 devices in a mesh: fsdp: 8 (over z, y), seq: 4 (over x, core).
Axes of the slice: x: 2, y: 2, z: 4, core: 2. Of those that a mesh axis runs over, the one named last changes fastest.
Arguments:
- block_in: float32 [16, 580, 768], P('fsdp', 'seq'), may hold values from -6 to 6
- teacher: float32 [16, 580, 768], P('fsdp', 'seq'), may hold values from -6 to 6
- image_counts: int32 [8], replicated, may hold values from 1 to 2, as said below
- expert_ids: int32 [4, 16, 145, 2], P('seq', 'fsdp'), may hold values from 0 to 3, all different within a row; in each aligned block of 290 rows (0 to 289, 290 to 579, ..., all dimensions but the last counted through in order) at most 164 rows name the same one
- pair_keep: int32 [4, 16, 145, 2], P('seq', 'fsdp'), may hold values 0 or 1
- norm1_gain: bfloat16 [768], P('fsdp'), may hold values from 0.25 to 1.75
- norm1_bias: bfloat16 [768], P('fsdp'), may hold values from -1.1953125 to 1.1953125
- qkv_weight: bfloat16 [768, 2304], P('fsdp'), may hold values from -0.3125 to 0.3125
- out_weight: bfloat16 [768, 768], P('fsdp'), may hold values from -0.5 to 0.5
- norm2_gain: bfloat16 [768], P('fsdp'), may hold values from 0.25 to 1.75
- norm2_bias: bfloat16 [768], P('fsdp'), may hold values from -1.1953125 to 1.1953125
- router_weight: bfloat16 [768, 4], P('fsdp'), may hold values from -0.15625 to 0.15625
- expert_in: bfloat16 [768, 4, 3072], P('fsdp'), may hold values from -0.21875 to 0.21875
- expert_out: bfloat16 [3072, 4, 768], P('fsdp'), may hold values from -0.625 to 0.625
Outputs:
- block_out: float32 [16, 580, 768], P('fsdp', 'seq')
- mean_loss: float32 [], replicated
- grad_block_in: float32 [16, 580, 768], P('fsdp', 'seq')
- grad_norm1_gain: float32 [768], P('fsdp')
- grad_norm1_bias: float32 [768], P('fsdp')
- grad_qkv_weight: float32 [768, 2304], P('fsdp')
- grad_out_weight: float32 [768, 768], P('fsdp')
- grad_norm2_gain: float32 [768], P('fsdp')
- grad_norm2_bias: float32 [768], P('fsdp')
- grad_router_weight: float32 [768, 4], P('fsdp')
- grad_expert_in: float32 [768, 4, 3072], P('fsdp')
- grad_expert_out: float32 [3072, 4, 768], P('fsdp')
Inputs may be any that keep to these rules, and one draw needn't show every extreme that they name: `image_counts`: some group holds 2 images. `expert_ids`: the 2 experts of a slot differ; in the slots of one device (aligned blocks of 290 rows, leading dimensions taken together in order) no expert is named by more than 164 rows, a bound that some block reaches.
All inputs are finite; a program needn't handle non-finite values. No bound on the sum of `pair_keep` on one device may be relied on, other than what follows from the above.
Results may differ from a plain program's by a relative error of at most 0.013.
The roundings to bfloat16 on the way count: a program that leaves them out, or rounds other values in their place, can miss the bound.
Values may be sent and summed in bfloat16 or wider, within the bound.
A program may use at most 320 MiB of HBM per device.

v0:
```python
import jax
import jax.numpy as jnp
from jax import lax
from jax.sharding import PartitionSpec as P

HEADS = 12
HD = 64
SEQ_LEN = 577
EXPERTS = 4
TOPK = 2


NORM_EPS = 1e-06
PRECISE = lax.Precision.HIGHEST


def layer_norm(values_in, gain_vec, bias_vec):
    centered = values_in - jnp.mean(values_in, axis=-1, keepdims=True)
    variance = jnp.mean(centered * centered, axis=-1, keepdims=True)
    return centered * lax.rsqrt(variance + NORM_EPS) * gain_vec + bias_vec


def slot_holds(piece_index, piece_len, seq_len, pieces):
    lengths = seq_len // pieces + (piece_index < seq_len % pieces).astype(jnp.int32)
    return jnp.arange(piece_len, dtype=jnp.int32)[None, :] < lengths[:, None]


def route_slots(expert_rows, usable, experts, capacity):
    expert_hits = (
        (expert_rows[:, :, None] == jnp.arange(experts, dtype=jnp.int32)[None, None, :])
        & usable[:, :, None]
    ).astype(jnp.int32)
    flat_hits = expert_hits.reshape(-1, experts)
    earlier = (jnp.cumsum(flat_hits, axis=0, dtype=jnp.int32) - flat_hits).reshape(
        expert_hits.shape
    )
    within = jnp.sum(earlier * expert_hits, axis=2, dtype=jnp.int32)
    return jnp.where(usable, expert_rows * capacity + within, experts * capacity)


def slot_pairs(slot_index, experts, capacity):
    pair_total = slot_index.size
    slot_table = jnp.full((experts * capacity + 1,), pair_total, jnp.int32)
    return slot_table.at[slot_index.reshape(-1)].set(jnp.arange(pair_total, dtype=jnp.int32))[
        : experts * capacity
    ]


def router_softmax(logit_rows):
    return jax.nn.softmax(logit_rows, axis=-1)


def exact_gelu(values_in):
    return jax.nn.gelu(values_in, approximate=False)


def finish_sums(owned_all):
    gain_one_o, bias_one_o, qkv_o, out_o, gain_two_o, bias_two_o, router_o, up_o, down_o = owned_all
    stacked = jnp.stack([gain_one_o, bias_one_o, gain_two_o, bias_two_o], axis=0)
    shares = (
        lax.psum_scatter(
            stacked.astype(jnp.bfloat16), "seq", scatter_dimension=0, tiled=True
        ).astype(jnp.float32),
        lax.psum_scatter(qkv_o.astype(jnp.bfloat16), "seq", scatter_dimension=1, tiled=True).astype(
            jnp.float32
        ),
        lax.psum_scatter(out_o.astype(jnp.bfloat16), "seq", scatter_dimension=1, tiled=True).astype(
            jnp.float32
        ),
        lax.psum_scatter(
            router_o.astype(jnp.bfloat16), "seq", scatter_dimension=1, tiled=True
        ).astype(jnp.float32),
        lax.psum_scatter(up_o.astype(jnp.bfloat16), "seq", scatter_dimension=2, tiled=True).astype(
            jnp.float32
        ),
        lax.psum_scatter(
            down_o.astype(jnp.bfloat16), "seq", scatter_dimension=2, tiled=True
        ).astype(jnp.float32),
    )
    whole = (
        lax.all_gather(shares[0].astype(jnp.bfloat16), "seq", axis=0, tiled=True).astype(
            jnp.float32
        ),
        lax.all_gather(shares[1].astype(jnp.bfloat16), "seq", axis=1, tiled=True).astype(
            jnp.float32
        ),
        lax.all_gather(shares[2].astype(jnp.bfloat16), "seq", axis=1, tiled=True).astype(
            jnp.float32
        ),
        lax.all_gather(shares[3].astype(jnp.bfloat16), "seq", axis=1, tiled=True).astype(
            jnp.float32
        ),
        lax.all_gather(shares[4].astype(jnp.bfloat16), "seq", axis=2, tiled=True).astype(
            jnp.float32
        ),
        lax.all_gather(shares[5].astype(jnp.bfloat16), "seq", axis=2, tiled=True).astype(
            jnp.float32
        ),
    )
    stats, qkv_s, out_s, router_s, up_s, down_s = whole
    return (stats[0], stats[1], qkv_s, out_s, stats[2], stats[3], router_s, up_s, down_s)


def on_device(
    block_in,
    teacher,
    image_counts,
    expert_ids,
    pair_keep,
    norm1_gain,
    norm1_bias,
    qkv_weight,
    out_weight,
    norm2_gain,
    norm2_bias,
    router_weight,
    expert_in,
    expert_out,
):
    image_count, piece_len, features = block_in.shape
    pieces = lax.axis_size("seq")
    seq_place = lax.axis_index("seq")
    group_place = lax.axis_index("fsdp")
    row_count = image_count * piece_len
    image_slots = pieces * piece_len
    heads_here = HEADS // pieces
    head_cols = heads_here * HD
    capacity = row_count * TOPK * 9 // (EXPERTS * 8) + 1
    inv_root = HD ** (-0.5)
    layer_full = (
        lax.all_gather(norm1_gain, "fsdp", axis=0, tiled=True),
        lax.all_gather(norm1_bias, "fsdp", axis=0, tiled=True),
        lax.all_gather(qkv_weight, "fsdp", axis=0, tiled=True),
        lax.all_gather(out_weight, "fsdp", axis=0, tiled=True),
        lax.all_gather(norm2_gain, "fsdp", axis=0, tiled=True),
        lax.all_gather(norm2_bias, "fsdp", axis=0, tiled=True),
        lax.all_gather(router_weight, "fsdp", axis=0, tiled=True),
    )
    expert_full = (
        lax.all_gather(expert_in, "fsdp", axis=0, tiled=True),
        lax.all_gather(expert_out, "fsdp", axis=0, tiled=True),
    )
    gain_one, bias_one, qkv_full, out_full, gain_two, bias_two, router_full = layer_full
    in_full, down_full = expert_full
    own_slots = slot_holds(jnp.reshape(seq_place, (1,)), piece_len, SEQ_LEN, pieces).reshape(
        piece_len
    )
    key_ok = slot_holds(jnp.arange(pieces, dtype=jnp.int32), piece_len, SEQ_LEN, pieces).reshape(
        image_slots
    )
    group_count = jnp.sum(
        jnp.where(
            jnp.arange(image_counts.shape[0], dtype=jnp.int32) == group_place, image_counts, 0
        )
    )
    token_ok = (
        (jnp.arange(image_count, dtype=jnp.int32) < group_count)[:, None] & own_slots[None, :]
    ).reshape(row_count)
    flat_in = block_in.reshape(row_count, features)
    normed_one, norm_one_back = jax.vjp(
        layer_norm, flat_in, gain_one.astype(jnp.float32), bias_one.astype(jnp.float32)
    )
    low_one = normed_one.astype(jnp.bfloat16)
    projected = jnp.dot(low_one, qkv_full, preferred_element_type=jnp.float32).astype(jnp.bfloat16)
    by_heads = lax.all_to_all(
        projected.reshape(image_count, piece_len, 3, pieces, head_cols),
        "seq",
        split_axis=3,
        concat_axis=1,
        tiled=True,
    )
    by_heads = by_heads.reshape(image_count, image_slots, 3, heads_here, HD)

    def masked_scores(queries, key_rows):
        scores = (
            jnp.einsum("qhd,khd->hqk", queries, key_rows, preferred_element_type=jnp.float32)
            * inv_root
        )
        return jnp.where(key_ok[None, None, :], scores, -1e30)

    def attend_one(image_block):
        queries, key_rows, value_rows = (image_block[:, 0], image_block[:, 1], image_block[:, 2])
        scores = masked_scores(queries, key_rows)
        highest = jnp.max(scores, axis=-1, keepdims=True)
        raised = jnp.exp(scores - highest)
        row_total = jnp.sum(raised, axis=-1, keepdims=True)
        shares = (raised / row_total).astype(jnp.bfloat16)
        context = jnp.einsum("hqk,khd->qhd", shares, value_rows, preferred_element_type=jnp.float32)
        return (context.astype(jnp.bfloat16), (highest + jnp.log(row_total))[:, :, 0])

    contexts, log_totals = lax.map(attend_one, by_heads)
    gathered_ctx = lax.all_to_all(
        contexts.reshape(image_count, image_slots, 1, head_cols),
        "seq",
        split_axis=1,
        concat_axis=2,
        tiled=True,
    )
    context_rows = gathered_ctx.reshape(row_count, features)
    attended = jnp.dot(context_rows, out_full, preferred_element_type=jnp.float32)
    middle = flat_in + attended
    normed_two, norm_two_back = jax.vjp(
        layer_norm, middle, gain_two.astype(jnp.float32), bias_two.astype(jnp.float32)
    )
    low_two = normed_two.astype(jnp.bfloat16)
    logits = jnp.dot(low_two, router_full, preferred_element_type=jnp.float32)
    routed, routed_back = jax.vjp(router_softmax, logits)
    expert_rows = expert_ids.reshape(row_count, TOPK)
    usable = (pair_keep.reshape(row_count, TOPK) == 1) & token_ok[:, None]
    slot_index = route_slots(expert_rows, usable, EXPERTS, capacity)
    pair_of_slot = slot_pairs(slot_index, EXPERTS, capacity)
    source_row = pair_of_slot // TOPK
    filled = source_row < row_count
    dispatched = jnp.where(
        filled[:, None],
        low_two[jnp.minimum(source_row, row_count - 1)],
        jnp.zeros((), jnp.bfloat16),
    )
    dispatched = dispatched.reshape(EXPERTS, capacity, features)
    hidden = jnp.einsum("ecd,def->ecf", dispatched, in_full, preferred_element_type=jnp.float32)
    activated, gelu_back = jax.vjp(exact_gelu, hidden)
    low_act = activated.astype(jnp.bfloat16)
    returned = jnp.einsum("ecf,fed->ecd", low_act, down_full, preferred_element_type=jnp.float32)
    flat_back = jnp.concatenate(
        [returned.reshape(EXPERTS * capacity, features), jnp.zeros((1, features), jnp.float32)],
        axis=0,
    )
    picked = flat_back[slot_index]
    chosen = expert_rows[:, :, None] == jnp.arange(EXPERTS, dtype=jnp.int32)[None, None, :]
    gate_values = jnp.sum(jnp.where(chosen, routed[:, None, :], 0.0), axis=2)
    pair_weight = jnp.where(usable, gate_values, 0.0)
    mixture = jnp.sum(pair_weight[:, :, None] * picked, axis=1)
    block_out = middle + mixture
    misfit = (block_out - teacher.reshape(row_count, features)) * token_ok.astype(jnp.float32)[
        :, None
    ]
    misfit_total = lax.psum(jnp.sum(misfit * misfit), ("fsdp", "seq"))
    mean_loss = misfit_total / (
        (jnp.sum(image_counts, dtype=jnp.int32) * SEQ_LEN).astype(jnp.float32) * features
    )
    later_layer = (
        lax.all_gather(qkv_weight, "fsdp", axis=0, tiled=True),
        lax.all_gather(out_weight, "fsdp", axis=0, tiled=True),
        lax.all_gather(router_weight, "fsdp", axis=0, tiled=True),
    )
    later_expert = (
        lax.all_gather(expert_in, "fsdp", axis=0, tiled=True),
        lax.all_gather(expert_out, "fsdp", axis=0, tiled=True),
    )
    qkv_back, out_back, router_back = later_layer
    in_back, down_back = later_expert
    pick_grad = pair_weight[:, :, None] * misfit[:, None, :]
    weight_grad = jnp.where(usable, jnp.sum(picked * misfit[:, None, :], axis=2), 0.0)
    pick_rows = jnp.concatenate(
        [pick_grad.reshape(row_count * TOPK, features), jnp.zeros((1, features), jnp.float32)],
        axis=0,
    )
    returned_grad = (
        pick_rows[pair_of_slot].reshape(EXPERTS, capacity, features).astype(jnp.bfloat16)
    )
    act_grad = jnp.einsum(
        "ecd,fed->ecf", returned_grad, down_back, preferred_element_type=jnp.float32
    )
    hidden_grad = gelu_back(act_grad)[0].astype(jnp.bfloat16)
    grad_down = jnp.einsum(
        "ecf,ecd->fed", low_act, returned_grad, preferred_element_type=jnp.float32
    )
    grad_up = jnp.einsum(
        "ecd,ecf->def", dispatched, hidden_grad, preferred_element_type=jnp.float32
    )
    dispatch_grad = jnp.einsum(
        "ecf,def->ecd", hidden_grad, in_back, preferred_element_type=jnp.float32
    )
    dispatch_rows = jnp.concatenate(
        [
            dispatch_grad.reshape(EXPERTS * capacity, features),
            jnp.zeros((1, features), jnp.float32),
        ],
        axis=0,
    )
    prob_grad = jnp.sum(jnp.where(chosen, weight_grad[:, :, None], 0.0), axis=1)
    logit_grad = routed_back(prob_grad)[0]
    grad_router = jnp.einsum(
        "rd,re->de", low_two.astype(jnp.float32), logit_grad, precision=PRECISE
    )
    normed_two_grad = jnp.sum(dispatch_rows[slot_index], axis=1) + jnp.einsum(
        "re,de->rd", logit_grad, router_back.astype(jnp.float32), precision=PRECISE
    )
    middle_ln_grad, gain_two_grad, bias_two_grad = norm_two_back(normed_two_grad)
    middle_grad = misfit + middle_ln_grad
    attended_grad = middle_grad.astype(jnp.bfloat16)
    grad_out_w = jnp.einsum(
        "rc,rd->cd", context_rows, attended_grad, preferred_element_type=jnp.float32
    )
    context_grad = jnp.einsum(
        "rd,cd->rc", attended_grad, out_back, preferred_element_type=jnp.float32
    ).astype(jnp.bfloat16)
    heads_grad = lax.all_to_all(
        context_grad.reshape(image_count, piece_len, pieces, head_cols),
        "seq",
        split_axis=2,
        concat_axis=1,
        tiled=True,
    )
    heads_grad = heads_grad.reshape(image_count, image_slots, heads_here, HD)

    def attend_back(image_item):
        image_block, out_grad, log_total = image_item
        queries, key_rows, value_rows = (image_block[:, 0], image_block[:, 1], image_block[:, 2])
        shares = jnp.exp(masked_scores(queries, key_rows) - log_total[:, :, None])
        value_grad = jnp.einsum(
            "hqk,qhd->khd",
            shares.astype(jnp.bfloat16),
            out_grad,
            preferred_element_type=jnp.float32,
        )
        share_grad = jnp.einsum(
            "qhd,khd->hqk", out_grad, value_rows, preferred_element_type=jnp.float32
        )
        score_grad = (
            shares * (share_grad - jnp.sum(shares * share_grad, axis=-1, keepdims=True))
        ).astype(jnp.bfloat16)
        query_grad = (
            jnp.einsum("hqk,khd->qhd", score_grad, key_rows, preferred_element_type=jnp.float32)
            * inv_root
        )
        key_grad = (
            jnp.einsum("hqk,qhd->khd", score_grad, queries, preferred_element_type=jnp.float32)
            * inv_root
        )
        return jnp.stack([query_grad, key_grad, value_grad], axis=1).astype(jnp.bfloat16)

    qkv_grads = lax.map(attend_back, (by_heads, heads_grad, log_totals))
    piece_grads = lax.all_to_all(
        qkv_grads.reshape(image_count, image_slots, 3, 1, head_cols),
        "seq",
        split_axis=1,
        concat_axis=3,
        tiled=True,
    )
    qkv_rows_grad = piece_grads.reshape(row_count, 3 * features)
    grad_qkv = jnp.einsum("rc,rd->cd", low_one, qkv_rows_grad, preferred_element_type=jnp.float32)
    normed_one_grad = jnp.einsum(
        "rd,cd->rc", qkv_rows_grad, qkv_back, preferred_element_type=jnp.float32
    )
    input_ln_grad, gain_one_grad, bias_one_grad = norm_one_back(normed_one_grad)
    input_grad = middle_grad + input_ln_grad
    layer_grads = (
        lax.psum_scatter(gain_one_grad, "fsdp", scatter_dimension=0, tiled=True),
        lax.psum_scatter(bias_one_grad, "fsdp", scatter_dimension=0, tiled=True),
        lax.psum_scatter(grad_qkv, "fsdp", scatter_dimension=0, tiled=True),
        lax.psum_scatter(grad_out_w, "fsdp", scatter_dimension=0, tiled=True),
        lax.psum_scatter(gain_two_grad, "fsdp", scatter_dimension=0, tiled=True),
        lax.psum_scatter(bias_two_grad, "fsdp", scatter_dimension=0, tiled=True),
        lax.psum_scatter(grad_router, "fsdp", scatter_dimension=0, tiled=True),
    )
    (
        owned_gain_one,
        owned_bias_one,
        owned_qkv,
        owned_out,
        owned_gain_two,
        owned_bias_two,
        owned_router,
    ) = layer_grads
    owned_up, owned_down = (
        lax.psum_scatter(grad_up, "fsdp", scatter_dimension=0, tiled=True),
        lax.psum_scatter(grad_down, "fsdp", scatter_dimension=0, tiled=True),
    )
    summed = finish_sums(
        (
            owned_gain_one,
            owned_bias_one,
            owned_qkv,
            owned_out,
            owned_gain_two,
            owned_bias_two,
            owned_router,
            owned_up,
            owned_down,
        )
    )
    return (
        block_out.reshape(image_count, piece_len, features),
        mean_loss,
        input_grad.reshape(image_count, piece_len, features),
        summed[0],
        summed[1],
        summed[2],
        summed[3],
        summed[4],
        summed[5],
        summed[6],
        summed[7],
        summed[8],
    )


def solution(mesh):
    return jax.shard_map(
        on_device,
        mesh=mesh,
        in_specs=(
            P("fsdp", "seq", None),
            P("fsdp", "seq", None),
            P(),
            P("seq", "fsdp", None, None),
            P("seq", "fsdp", None, None),
            P("fsdp"),
            P("fsdp"),
            P("fsdp", None),
            P("fsdp", None),
            P("fsdp"),
            P("fsdp"),
            P("fsdp", None),
            P("fsdp", None, None),
            P("fsdp", None, None),
        ),
        out_specs=(
            P("fsdp", "seq", None),
            P(),
            P("fsdp", "seq", None),
            P("fsdp"),
            P("fsdp"),
            P("fsdp", None),
            P("fsdp", None),
            P("fsdp"),
            P("fsdp"),
            P("fsdp", None),
            P("fsdp", None, None),
            P("fsdp", None, None),
        ),
        check_vma=False,
    )
```

profile of v0, /device:TPU:25, one launch (start us, length us, event | category | flops | bytes accessed | tf_op | source)
XLA Modules:
  0.0 3298.4 jit_solution(10133413761269367991)
XLA Ops:
  16.5 15.1 all-reduce.16
  34.3 41.3 %all-gather.11.cloned.1.call-done = bf16[768,2304]{1,0:T(8,128)(2,1)} async-done(((bf16[96,2304]{1,0:T(8,128)(2,1)}), bf16[768,2304]{1,0:T(8,128)(2,1)}) %all-gather.11.cloned.1.call-update) | async-done | bytes 3538960 | tf_op jit(solution)/shard_map/all_gather | solution.py:133
  85.9 5.3 all-to-all-start
  92.6 20.1 all-to-all-done
  112.8 8.8 copy.260
  121.5 4.1 reshape.544
  125.7 7.3 while.24
  134.4 5.0 all-to-all-start.1
  141.8 18.8 all-gather
  171.7 4.3 scatter_custom_fusion
  182.8 299.7 %all-gather.15.cloned.1.call-done = bf16[768,4,3072]{2,0,1:T(8,128)(2,1)} async-done(((bf16[96,4,3072]{2,0,1:T(8,128)(2,1)}), bf16[768,4,3072]{2,0,1:T(8,128)(2,1)}) %all-gather.15.cloned.1.call-update) | async-done | bytes 18874384 | tf_op jit(solution)/shard_map/all_gather | solution.py:140
  482.5 10.5 fusion.44
  496.2 19.6 multiply_convert_fusion.1
  515.8 330.6 %all-gather.17.cloned.1.call-done = bf16[3072,4,768]{2,0,1:T(8,128)(2,1)} async-done(((bf16[384,4,768]{2,0,1:T(8,128)(2,1)}), bf16[3072,4,768]{2,0,1:T(8,128)(2,1)}) %all-gather.17.cloned.1.call-update) | async-done | bytes 18874384 | tf_op jit(solution)/shard_map/all_gather | solution.py:141
  846.3 12.3 fusion.89
  887.2 17.2 convolution_bitcast_fusion
  908.8 14.9 add_convert_fusion
  925.8 11.7 fusion.90
  949.0 4.7 reduce_sum.281
  966.8 4.9 all-to-all-done.2
  974.0 16.3 while.25
  990.2 5.3 copy.285
  995.5 4.3 all-to-all-start.3
  999.8 17.5 convolution_bitcast_fusion.1
  1017.3 44.9 %copy.292 = f32[768,4,3072]{2,1,0:T(4,128)} copy(f32[768,4,3072]{0,2,1:T(8,128)} %convolution_bitcast_fusion.1) | data formatting | bytes 75497472 | tf_op jit(solution)/shard_map/ecd,ecf->def/transpose | solution.py:268
  1066.3 4.9 multiply_reduce_fusion.4
  1071.2 1644.1 %all-reduce.19 = (bf16[768]{0:T(1024)(128)(2,1)S(1)}, bf16[768]{0:T(1024)(128)(2,1)S(1)}, bf16[768]{0:T(1024)(128)(2,1)S(1)}, bf16[768]{0:T(1024)(128)(2,1)S(1)}, bf16[768,4,3072]{2,1,0:T(4,128)(2,1)}) all-reduce(f32[768]{0:T(1024)S(1)} %get-tuple-element.194, ...), channel_id=5, replica_groups=mesh['fsdp'=8,'seq'=4] {'fsdp'}, use_global_device_ids=true, to_apply=%region_38.39.clone | all-reduce | flops 9440256 | bytes 56641536
  2717.8 60.9 %copy.309 = bf16[96,4,3072]{1,0,2:T(8,128)(2,1)} copy(bf16[96,4,3072]{2,1,0:T(4,128)(2,1)S(1)} %dynamic-slice_convert_fusion) | data formatting | bytes 4718592
  2778.7 139.9 %reshape.650 = bf16[3072,384]{1,0:T(8,128)(2,1)} reshape(bf16[3072,96,4]{2,1,0:T(8,128)(2,1)} %bitcast.54) | data formatting | bytes 4718592
  2920.7 6.0 fusion.91
  2926.8 4.6 convert_element_type.172
  2935.1 18.0 reduce-scatter.31.cloned.1.call-done
  2953.1 41.3 %reshape.651 = bf16[768,96,4]{2,1,0:T(8,128)(2,1)} reshape(bf16[768,384]{1,0:T(8,128)(2,1)} %reduce-scatter.31.cloned.1.call-done) | data formatting | bytes 1179648
  2994.4 22.8 copy.310
  3017.3 67.1 %reduce-scatter.17.cloned.1.call-done = f32[96,2304]{1,0:T(8,128)} async-done(((f32[768,2304]{1,0:T(8,128)}), f32[96,2304]{1,0:T(8,128)}) %reduce-scatter.17.cloned.1.call-update) | async-done | bytes 884752 | tf_op jit(solution)/shard_map/reduce_scatter | solution.py:351
  3086.8 33.9 %reduce-scatter.23.cloned.1.call-done = bf16[384,4,192]{0,2,1:T(8,128)(2,1)} async-done(((bf16[384,4,768]{0,2,1:T(8,128)(2,1)}), bf16[384,4,192]{0,2,1:T(8,128)(2,1)}) %reduce-scatter.23.cloned.1.call-update) | async-done | bytes 589840 | tf_op jit(solution)/shard_map/reduce_scatter | solution.py:76
  3122.0 38.2 %psum.7 = f32[]{:T(128)} all-reduce(f32[]{:T(128)} %get-tuple-element.236), channel_id=1, replica_groups=mesh['fsdp'=8,'seq'=4] {'fsdp','seq'}, use_global_device_ids=true, to_apply=%region_18.19 | all-reduce | flops 1 | bytes 8 | tf_op jit(solution)/shard_map/psum | solution.py:237
  3163.5 19.3 reduce-scatter.29.cloned.1.call-done
  3187.2 7.9 all-reduce.17
  3195.7 5.5 all-gather.3
  3202.5 5.0 all-gather.1
  3208.0 6.0 all_gather.61
  3214.9 19.3 all-gather.19.cloned.1.call-done
  3234.2 5.2 convert_element_type.171
  3239.5 19.6 reduce-scatter.25.cloned.1.call-done
  3260.1 7.1 all-gather.2
  3269.0 16.0 all-gather.21.cloned.1.call-done
  3284.9 5.6 copy.296
  (415 shorter events, 159.6 us)
Async XLA Ops:
  7.2 68.4 %all-gather.11.cloned.1.call-start = ((), (), s32[]{:S(2)}) async-start(), calls=%async_computation.12 | async-start | bytes 3981312 | tf_op jit(solution)/shard_map/all_gather | solution.py:133
  7.9 157.4 %all-gather.13.cloned.1.call-start = ((), (), s32[]{:S(2)}) async-start(), calls=%async_computation.13 | async-start | bytes 1327104 | tf_op jit(solution)/shard_map/all_gather | solution.py:134
  8.7 473.8 %all-gather.15.cloned.1.call-start = ((), (), s32[]{:S(2)}) async-start(), calls=%async_computation.14 | async-start | bytes 21233664 | tf_op jit(solution)/shard_map/all_gather | solution.py:140
  12.5 19.2 copy-start.11
  12.6 833.8 %all-gather.17.cloned.1.call-start = ((), (), s32[]{:S(2)}) async-start(), calls=%async_computation.15 | async-start | bytes 21233664 | tf_op jit(solution)/shard_map/all_gather | solution.py:141
  31.7 47.2 %copy-start.59 = (f32[768]{0:T(1024)}, f32[768]{0:T(1024)S(1)}, u32[]{:S(2)}) copy-start(f32[768]{0:T(1024)S(1)} %convert_element_type.144) | copy-start | bytes 9220
  31.7 47.2 %copy-start.44 = (f32[768]{0:T(1024)}, f32[768]{0:T(1024)S(1)}, u32[]{:S(2)}) copy-start(f32[768]{0:T(1024)S(1)} %convert_element_type.143) | copy-start | bytes 9220
  32.3 46.6 %copy-start.68 = (f32[290]{0:T(512)}, f32[290]{0:T(512)S(1)}, u32[]{:S(2)}) copy-start(f32[290]{0:T(512)S(1)} %div.88) | copy-start | bytes 3484
  33.7 45.2 %copy-start.70 = (f32[290]{0:T(512)}, f32[290]{0:T(512)S(1)}, u32[]{:S(2)}) copy-start(f32[290]{0:T(512)S(1)} %rsqrt.23) | copy-start | bytes 3484
  34.3 131.1 %copy-start.14 = (f32[290,768]{1,0:T(8,128)}, f32[290,768]{1,0:T(8,128)S(1)}, u32[]{:S(2)}) copy-start(f32[290,768]{1,0:T(8,128)S(1)} %reshape.542) | copy-start | bytes 2672644
  79.0 12.3 copy-start.75
  79.0 13.6 copy-start.72
  85.9 26.9 all-to-all-start
  125.7 15.6 copy-start.46
  125.7 16.1 copy-start.74
  134.4 28.9 all-to-all-start.1
  139.4 2787.4 %reduce-scatter.21.cloned.1.call-start = ((), (), s32[]{:S(2)}) async-start(), calls=%async_computation.19 | async-start | bytes 42467328 | tf_op jit(solution)/shard_map/reduce_scatter | solution.py:368
  139.6 36.9 %copy-start.62 = (pred[290,2]{0,1:T(4,128)(4,1)}, pred[290,2]{0,1:T(4,128)(4,1)S(1)}, u32[]{:S(2)}) copy-start(pred[290,2]{0,1:T(4,128)(4,1)S(1)} %eq.90) | copy-start | bytes 1744
  140.2 36.2 %copy-start.64 = (pred[290]{0:T(512)(128)(4,1)}, pred[290]{0:T(512)(128)(4,1)S(1)}, u32[]{:S(2)}) copy-start(pred[290]{0:T(512)(128)(4,1)S(1)} %and.98) | copy-start | bytes 874
  141.6 26.1 copy-start.35
  141.8 27.2 copy-start.49
  165.3 12.6 copy-start.21
  167.4 13.9 copy-start.42
  168.6 12.7 copy-start
  168.9 784.8 %copy-start.27 = (f32[290,4]{0,1:T(4,128)}, f32[290,4]{0,1:T(4,128)S(1)}, u32[]{:S(2)}) copy-start(f32[290,4]{0,1:T(4,128)S(1)} %get-tuple-element.259) | copy-start | bytes 13924
  168.9 735.5 %copy-start.39 = (f32[290]{0:T(512)}, f32[290]{0:T(512)S(1)}, u32[]{:S(2)}) copy-start(f32[290]{0:T(512)S(1)} %fusion.80) | copy-start | bytes 3484
  182.7 310.3 %copy-start.18 = (bf16[4,164,768]{2,1,0:T(8,128)(2,1)}, bf16[4,164,768]{2,1,0:T(8,128)(2,1)S(1)}, u32[]{:S(2)}) copy-start(bf16[4,164,768]{2,1,0:T(8,128)(2,1)S(1)} %gather.15) | copy-start | bytes 3022852
  182.7 310.2 %copy-start.51 = (pred[4,164]{1,0:T(4,128)(4,1)}, pred[4,164]{1,0:T(4,128)(4,1)S(1)}, u32[]{:S(2)}) copy-start(pred[4,164]{1,0:T(4,128)(4,1)S(1)} %fusion.60) | copy-start | bytes 1972
  887.1 17.2 copy-start.20
  908.2 45.5 %copy-start.29 = (f32[290,4]{0,1:T(4,128)}, f32[290,4]{0,1:T(4,128)S(1)}, u32[]{:S(2)}) copy-start(f32[290,4]{0,1:T(4,128)S(1)} %select_reduce_fusion) | copy-start | bytes 13924
  959.0 12.7 all-to-all-start.2
  962.8 1970.4 %reduce-scatter.19.cloned.1.call-start = ((), (), s32[]{:S(2)}) async-start(), calls=%async_computation.17 | async-start | bytes 2654208 | tf_op jit(solution)/shard_map/reduce_scatter | solution.py:352
  995.5 66.7 %all-to-all-start.3 = ((bf16[2,580,3,1,192]{4,0,3,2,1:T(2,128)(2,1)}), bf16[2,580,3,1,192]{4,0,3,2,1:T(2,128)(2,1)S(1)}, u32[]{:S(2)}, u32[]{:S(2)}) async-start(bf16[2,580,3,1,192]{4,0,3,2,1:T(2,128)(2,1)} %copy.285), calls=%async_computation.3 | async-start | bytes 3563520 | tf_op jit(solution)/shard_map/all_to_all | solution.py:334
  999.7 1953.3 %reduce-scatter.31.cloned.1.call-start = ((), (), s32[]{:S(2)}) async-start(), calls=%async_computation.25 | async-start | bytes 2949120
  2778.7 140.1 %copy-start.67 = (f32[2,145]{1,0:T(2,128)S(1)}, f32[2,145]{1,0:T(2,128)}, u32[]{:S(2)}) copy-start(f32[2,145]{1,0:T(2,128)} %get-tuple-element.252) | copy-start | bytes 3484
  2778.7 140.3 %copy-start.12 = (f32[2,145,768]{2,0,1:T(2,128)S(1)}, f32[2,145,768]{2,0,1:T(2,128)}, u32[]{:S(2)}) copy-start(f32[2,145,768]{2,0,1:T(2,128)} %param.18) | copy-start | bytes 2672644
  2778.7 140.3 %copy-start.26 = (f32[2,145]{0,1:T(8,128)S(1)}, f32[2,145]{0,1:T(8,128)}, u32[]{:S(2)}) copy-start(f32[2,145]{0,1:T(8,128)} %copy-done.25) | copy-start | bytes 3484
  2778.7 140.3 %copy-start.60 = (f32[768]{0:T(1024)S(1)}, f32[768]{0:T(1024)}, u32[]{:S(2)}) copy-start(f32[768]{0:T(1024)} %copy-done.59) | copy-start | bytes 9220
  2918.6 165.8 %reduce-scatter.17.cloned.1.call-start = ((), (), s32[]{:S(2)}) async-start(), calls=%async_computation.16 | async-start | bytes 7962624 | tf_op jit(solution)/shard_map/reduce_scatter | solution.py:351
  2926.7 193.9 %reduce-scatter.23.cloned.1.call-start = ((), (), s32[]{:S(2)}) async-start(), calls=%async_computation.20 | async-start | bytes 2949120 | tf_op jit(solution)/shard_map/reduce_scatter | solution.py:76
  2931.5 251.3 %reduce-scatter.29.cloned.1.call-start = ((), (), s32[]{:S(2)}) async-start(), calls=%async_computation.24 | async-start | bytes 442368
  2933.1 274.9 %reduce-scatter.27.cloned.1.call-start = ((), (), s32[]{:S(2)}) async-start(), calls=%async_computation.23 | async-start | bytes 245760
  2935.0 299.2 %all-gather.19.cloned.1.call-start = ((), (), s32[]{:S(2)}) async-start(), calls=%async_computation.18 | async-start | bytes 2949120 | tf_op jit(solution)/shard_map/all_gather | solution.py:93
  2994.4 126.3 %copy-start.80 = (u32[32]{0:T(128)S(1)}, u32[32]{0:T(128)}, u32[]{:S(2)}) copy-start(u32[32]{0:T(128)} %constant.239) | copy-start | bytes 388
  3017.3 166.4 %copy-start.58 = (f32[290]{0:T(512)S(1)}, f32[290]{0:T(512)}, u32[]{:S(2)}) copy-start(f32[290]{0:T(512)} %copy-done.57) | copy-start | bytes 3484
  3017.3 241.7 %reduce-scatter.25.cloned.1.call-start = ((), (), s32[]{:S(2)}) async-start(), calls=%async_computation.22 | async-start | bytes 737280
  3085.7 99.6 %copy-start.8 = (f32[290,768]{1,0:T(8,128)S(1)}, f32[290,768]{1,0:T(8,128)}, u32[]{:S(2)}) copy-start(f32[290,768]{1,0:T(8,128)} %copy-done.7) | copy-start | bytes 2672644
  3086.7 198.2 %all-gather.21.cloned.1.call-start = ((), (), s32[]{:S(2)}) async-start(), calls=%async_computation.21 | async-start | bytes 2949120 | tf_op jit(solution)/shard_map/all_gather | solution.py:96
  (55 other events, 271.3 us)
Sparse Core Ops, SparseCore 0:
  10.2 65.3 all-gather.10
  77.8 38.3 all-gather.12
  118.3 364.1 all-gather.14
  483.9 362.4 all-gather.16
  904.6 1063.5 reduce-scatter.20
  1972.4 178.3 reduce-scatter.18
  2918.8 34.2 reduce-scatter.30
  2956.8 127.6 reduce-scatter.16
  3087.1 33.5 reduce-scatter.22
  3124.4 58.3 reduce-scatter.28
  3185.8 21.7 reduce-scatter.26
  3209.6 24.5 all-gather.18
  3237.3 21.6 reduce-scatter.24
  3260.4 24.4 all-gather.20
where the time goes:
time: 3310 us; the launch traced here: 3300 us
  blocking collectives  1750 us (53%)
  waiting for transfers between devices  891 us (27%)
  local copies, waits for them, and re-layouts  435 us (13%)
  matrix products  123 us (4%)
  other arithmetic  62.8 us (2%)
    unnamed x3, blocking collectives  1670 us
    all_gather x1, waiting for transfers between devices, on_device(): lax.all_gather(expert_out, 'fsdp', axis=0, tiled=True)  331 us
    all_gather x1, waiting for transfers between devices, on_device(): lax.all_gather(expert_in, 'fsdp', axis=0, tiled=True)  300 us
    unnamed x195, local copies, waits for them, and re-layouts  297 us
    reduce_scatter x1, waiting for transfers between devices, on_device(): lax.psum_scatter(grad_qkv, 'fsdp', scatter_dimension=0, tiled=True)  67.1 us
  transfers between devices with their start and end apart: 18, of which 12 were waited for; matrix products, arithmetic and copies ran while one was open for 17% of the time, Pallas kernels for 0%

commit v1 on v0

v1 whole, which is shorter than its diff:
```python
import jax
import jax.numpy as jnp
from jax import lax
from jax.sharding import PartitionSpec as P

HEADS = 12
HD = 64
SEQ_LEN = 577
EXPERTS = 4
TOPK = 2
NORM_EPS = 1e-06
PRECISE = lax.Precision.HIGHEST
F32 = jnp.float32
BF16 = jnp.bfloat16


def layer_norm(values_in, gain_vec, bias_vec):
    centered = values_in - jnp.mean(values_in, axis=-1, keepdims=True)
    variance = jnp.mean(centered * centered, axis=-1, keepdims=True)
    root = lax.rsqrt(variance + NORM_EPS)
    unit = centered * root
    return unit * gain_vec + bias_vec, unit, root


def layer_norm_back(grad_out, unit, root, gain_vec):
    scaled = grad_out * gain_vec
    return root * (
        scaled
        - jnp.mean(scaled, axis=-1, keepdims=True)
        - unit * jnp.mean(scaled * unit, axis=-1, keepdims=True)
    )


def slot_holds(piece_index, piece_len, seq_len, pieces):
    lengths = seq_len // pieces + (piece_index < seq_len % pieces).astype(jnp.int32)
    return jnp.arange(piece_len, dtype=jnp.int32)[None, :] < lengths[:, None]


def dot32(left, right, dims):
    return lax.dot_general(left, right, (dims, ((), ())), preferred_element_type=F32)


def on_device(
    block_in,
    teacher,
    image_counts,
    expert_ids,
    pair_keep,
    norm1_gain,
    norm1_bias,
    qkv_weight,
    out_weight,
    norm2_gain,
    norm2_bias,
    router_weight,
    expert_in,
    expert_out,
):
    images, piece_len, features = block_in.shape
    pieces = lax.axis_size("seq")
    groups = lax.axis_size("fsdp")
    seq_place = lax.axis_index("seq")
    group_place = lax.axis_index("fsdp")
    rows = images * piece_len
    slots = pieces * piece_len
    heads_here = HEADS // pieces
    cols = heads_here * HD
    hidden_size = expert_in.shape[2]
    capacity = rows * TOPK * 9 // (EXPERTS * 8) + 1
    inv_root = HD ** (-0.5)
    in_rows = expert_in.shape[0]
    out_rows = expert_out.shape[0]

    small = jnp.concatenate(
        [
            jnp.stack([norm1_gain, norm1_bias, norm2_gain, norm2_bias], axis=1),
            router_weight,
            out_weight,
            lax.dynamic_index_in_dim(
                qkv_weight.reshape(-1, 3, pieces, cols), seq_place, 2, keepdims=False
            ).reshape(-1, 3 * cols),
        ],
        axis=1,
    )
    small_full = lax.all_gather(small, "fsdp", axis=0, tiled=True)
    gain_one, bias_one, gain_two, bias_two = [small_full[:, i].astype(F32) for i in range(4)]
    router_full = small_full[:, 4 : 4 + EXPERTS]
    out_full = small_full[:, 4 + EXPERTS : 4 + EXPERTS + features]
    qkv_here = small_full[:, 4 + EXPERTS + features :]
    up_here = lax.all_gather(
        lax.dynamic_index_in_dim(expert_in, seq_place, 1, keepdims=False), "fsdp", axis=0, tiled=True
    )
    down_here = lax.all_gather(
        lax.dynamic_index_in_dim(expert_out, seq_place, 1, keepdims=False), "fsdp", axis=0, tiled=True
    )

    own_slots = slot_holds(jnp.reshape(seq_place, (1,)), piece_len, SEQ_LEN, pieces).reshape(piece_len)
    key_ok = slot_holds(jnp.arange(pieces, dtype=jnp.int32), piece_len, SEQ_LEN, pieces).reshape(slots)
    group_count = jnp.sum(
        jnp.where(jnp.arange(image_counts.shape[0], dtype=jnp.int32) == group_place, image_counts, 0)
    )
    token_ok = (
        (jnp.arange(images, dtype=jnp.int32) < group_count)[:, None] & own_slots[None, :]
    ).reshape(rows)

    flat_in = block_in.reshape(rows, features)
    normed_one, unit_one, root_one = layer_norm(flat_in, gain_one, bias_one)
    low_one = normed_one.astype(BF16)
    low_all = lax.all_gather(low_one.reshape(images, piece_len, features), "seq", axis=1, tiled=True)
    projected = dot32(low_all, qkv_here, ((2,), (0,))).astype(BF16)
    by_heads = projected.reshape(images, slots, 3, heads_here, HD).transpose(2, 0, 3, 1, 4)
    queries, key_rows, value_rows = by_heads[0], by_heads[1], by_heads[2]
    scores = jnp.einsum("ihqd,ihkd->ihqk", queries, key_rows, preferred_element_type=F32) * inv_root
    scores = jnp.where(key_ok[None, None, None, :], scores, -1e30)
    raised = jnp.exp(scores - jnp.max(scores, axis=-1, keepdims=True))
    attn = raised / jnp.sum(raised, axis=-1, keepdims=True)
    attn_low = attn.astype(BF16)
    context = jnp.einsum("ihqk,ihkd->iqhd", attn_low, value_rows, preferred_element_type=F32).astype(BF16)
    context_rows = lax.all_to_all(
        context.reshape(images, slots, 1, cols), "seq", split_axis=1, concat_axis=2, tiled=True
    ).reshape(rows, features)
    middle = flat_in + dot32(context_rows, out_full, ((1,), (0,)))
    normed_two, unit_two, root_two = layer_norm(middle, gain_two, bias_two)
    low_two = normed_two.astype(BF16)
    probs = jax.nn.softmax(dot32(low_two, router_full, ((1,), (0,))), axis=-1)

    expert_rows = expert_ids.reshape(rows, TOPK)
    usable = (pair_keep.reshape(rows, TOPK) == 1) & token_ok[:, None]
    hit = jnp.any(
        (expert_rows[:, :, None] == jnp.arange(EXPERTS, dtype=jnp.int32)) & usable[:, :, None], axis=1
    )
    earlier = (jnp.arange(rows)[:, None] > jnp.arange(rows)[None, :]).astype(BF16)
    place = dot32(earlier, hit.astype(BF16), ((1,), (0,))).astype(jnp.int32)
    place = jnp.where(hit, place, -1)
    select = (place.T[:, None, :] == jnp.arange(capacity, dtype=jnp.int32)[None, :, None]).astype(BF16)
    weight = jnp.where(hit, probs, 0.0)

    dispatched = dot32(select, low_two, ((2,), (0,))).astype(BF16)
    arrived = lax.all_to_all(dispatched, "seq", split_axis=0, concat_axis=0, tiled=True)
    arrived = arrived.reshape(pieces * capacity, features)
    hidden = dot32(arrived, up_here, ((1,), (0,)))
    activated, gelu_back = jax.vjp(lambda u: jax.nn.gelu(u, approximate=False), hidden)
    low_act = activated.astype(BF16)
    returned = dot32(low_act, down_here, ((1,), (0,))).astype(BF16)
    returned = lax.all_to_all(
        returned.reshape(pieces, capacity, features), "seq", split_axis=0, concat_axis=0, tiled=True
    )
    picked = jnp.einsum("est,esd->etd", select, returned, preferred_element_type=F32)
    block_out = middle + jnp.sum(weight.T[:, :, None] * picked, axis=0)
    misfit = (block_out - teacher.reshape(rows, features)) * token_ok.astype(F32)[:, None]
    loss_here = jnp.sum(misfit * misfit)

    pair_grad = (weight.T[:, :, None] * misfit[None]).astype(BF16)
    returned_grad = jnp.einsum("est,etd->esd", select, pair_grad, preferred_element_type=F32).astype(BF16)
    prob_grad = jnp.where(hit, jnp.sum(picked * misfit[None], axis=2).T, 0.0)
    grad_arrived = lax.all_to_all(returned_grad, "seq", split_axis=0, concat_axis=0, tiled=True).reshape(
        pieces * capacity, features
    )
    hidden_grad = gelu_back(dot32(grad_arrived, down_here, ((1,), (1,))))[0].astype(BF16)
    grad_down = dot32(low_act, grad_arrived, ((0,), (0,))).astype(BF16)
    grad_up = dot32(arrived, hidden_grad, ((0,), (0,))).astype(BF16)
    dispatch_grad = dot32(hidden_grad, up_here, ((1,), (1,))).astype(BF16)
    dispatch_grad = lax.all_to_all(
        dispatch_grad.reshape(pieces, capacity, features), "seq", split_axis=0, concat_axis=0, tiled=True
    )
    owned_down = lax.psum_scatter(grad_down, "fsdp", scatter_dimension=0, tiled=True)
    owned_up = lax.psum_scatter(grad_up, "fsdp", scatter_dimension=0, tiled=True)

    logit_grad = probs * (prob_grad - jnp.sum(probs * prob_grad, axis=1, keepdims=True))
    grad_router = lax.dot_general(
        low_two.astype(F32), logit_grad, (((0,), (0,)), ((), ())), precision=PRECISE
    )
    normed_two_grad = jnp.einsum("est,esd->td", select, dispatch_grad, preferred_element_type=F32)
    normed_two_grad = normed_two_grad + lax.dot_general(
        logit_grad, router_full.astype(F32), (((1,), (1,)), ((), ())), precision=PRECISE
    )
    grad_gain_two = jnp.sum(normed_two_grad * unit_two, axis=0)
    grad_bias_two = jnp.sum(normed_two_grad, axis=0)
    middle_grad = misfit + layer_norm_back(normed_two_grad, unit_two, root_two, gain_two)
    attended_grad = middle_grad.astype(BF16)
    grad_out_w = dot32(context_rows, attended_grad, ((0,), (0,))).astype(BF16)
    context_grad = dot32(attended_grad, out_full, ((1,), (1,))).astype(BF16)
    heads_grad = lax.all_to_all(
        context_grad.reshape(images, piece_len, pieces, cols), "seq", split_axis=2, concat_axis=1, tiled=True
    ).reshape(images, slots, heads_here, HD)
    value_grad = jnp.einsum("ihqk,iqhd->ikhd", attn_low, heads_grad, preferred_element_type=F32)
    share_grad = jnp.einsum("iqhd,ihkd->ihqk", heads_grad, value_rows, preferred_element_type=F32)
    score_grad = (attn * (share_grad - jnp.sum(attn * share_grad, axis=-1, keepdims=True))).astype(BF16)
    query_grad = jnp.einsum("ihqk,ihkd->iqhd", score_grad, key_rows, preferred_element_type=F32) * inv_root
    key_grad = jnp.einsum("ihqk,ihqd->ikhd", score_grad, queries, preferred_element_type=F32) * inv_root
    heads_back = jnp.stack([query_grad, key_grad, value_grad], axis=2).astype(BF16)
    heads_back = heads_back.reshape(images * slots, 3 * cols)
    grad_qkv = dot32(low_all.reshape(images * slots, features), heads_back, ((0,), (0,))).astype(BF16)
    normed_one_part = dot32(heads_back, qkv_here, ((1,), (1,))).astype(BF16)
    normed_one_grad = lax.psum_scatter(
        normed_one_part.reshape(images, slots, features), "seq", scatter_dimension=1, tiled=True
    ).astype(F32).reshape(rows, features)
    grad_gain_one = jnp.sum(normed_one_grad * unit_one, axis=0)
    grad_bias_one = jnp.sum(normed_one_grad, axis=0)
    input_grad = middle_grad + layer_norm_back(normed_one_grad, unit_one, root_one, gain_one)

    out_share = lax.psum_scatter(grad_out_w, "seq", scatter_dimension=1, tiled=True)
    attn_owned = lax.psum_scatter(
        jnp.concatenate([grad_qkv, out_share], axis=1), "fsdp", scatter_dimension=0, tiled=True
    )
    loss_row = jnp.zeros((features,), F32).at[0].set(loss_here)
    vectors = jnp.concatenate(
        [jnp.stack([grad_gain_one, grad_bias_one, grad_gain_two, grad_bias_two, loss_row]), grad_router.T], axis=0
    )
    vectors = lax.psum(vectors, ("fsdp", "seq"))
    mean_loss = vectors[4, 0] / (
        (jnp.sum(image_counts, dtype=jnp.int32) * SEQ_LEN).astype(F32) * features
    )
    owned_vectors = lax.dynamic_slice_in_dim(vectors, group_place * in_rows, in_rows, axis=1)
    attn_whole = lax.all_gather(attn_owned, "seq", axis=0)
    grad_qkv_w = (
        attn_whole[:, :, : 3 * cols].reshape(pieces, in_rows, 3, cols).transpose(1, 2, 0, 3)
        .reshape(in_rows, 3 * features).astype(F32)
    )
    grad_out_whole = attn_whole[:, :, 3 * cols :].transpose(1, 0, 2).reshape(in_rows, features).astype(F32)
    grad_up_w = lax.all_gather(owned_up, "seq", axis=0).transpose(1, 0, 2).astype(F32)
    grad_down_w = lax.all_gather(owned_down, "seq", axis=0).transpose(1, 0, 2).astype(F32)
    return (
        block_out.reshape(images, piece_len, features),
        mean_loss,
        input_grad.reshape(images, piece_len, features),
        owned_vectors[0],
        owned_vectors[1],
        grad_qkv_w,
        grad_out_whole,
        owned_vectors[2],
        owned_vectors[3],
        owned_vectors[5:].T,
        grad_up_w,
        grad_down_w,
    )


def solution(mesh):
    return jax.shard_map(
        on_device,
        mesh=mesh,
        in_specs=(
            P("fsdp", "seq", None),
            P("fsdp", "seq", None),
            P(),
            P("seq", "fsdp", None, None),
            P("seq", "fsdp", None, None),
            P("fsdp"),
            P("fsdp"),
            P("fsdp", None),
            P("fsdp", None),
            P("fsdp"),
            P("fsdp"),
            P("fsdp", None),
            P("fsdp", None, None),
            P("fsdp", None, None),
        ),
        out_specs=(
            P("fsdp", "seq", None),
            P(),
            P("fsdp", "seq", None),
            P("fsdp"),
            P("fsdp"),
            P("fsdp", None),
            P("fsdp", None),
            P("fsdp"),
            P("fsdp"),
            P("fsdp", None),
            P("fsdp", None, None),
            P("fsdp", None, None),
        ),
        check_vma=False,
    )
```

time: 3310 us -> 769 us (0.23)
  blocking collectives: 1750 us -> 95.4 us
  waiting for transfers between devices: 891 us -> 387 us
  local copies, waits for them, and re-layouts: 435 us -> 91.7 us
    unnamed x3 -> x0, blocking collectives: 1670 us -> none
    all_gather x6, waiting for transfers between devices: 707 us -> 177 us  [the longest x1 57.3 us: on_device(): lax.all_gather(lax.dynamic_index_in_dim(expert_out, seq_place, 1, keepdim...]
    unnamed x195 -> x85, local copies, waits for them, and re-layouts: 297 us -> 16.1 us
    reduce_scatter x1, waiting for transfers between devices: 0.02 us -> 99.7 us  [on_device(): lax.psum_scatter(grad_down, 'fsdp', scatter_dimension=0, tiled=True)]
    reduce_scatter x3, waiting for transfers between devices: 101 us -> 40.5 us  [the longest x1 27.2 us: on_device(): lax.psum_scatter(grad_up, 'fsdp', scatter_dimension=0, tiled=True)]
    all_to_all x0 -> x3, blocking collectives: none -> 46.9 us  [the longest x1 17.5 us: on_device(): lax.all_to_all(returned_grad, 'seq', split_axis=0, concat_axis=0, tiled=T...]
    transpose x1, local copies, waits for them, and re-layouts: 44.9 us -> 0.66 us  [on_device(): owned_vectors[5:]]
    dot_general x28 -> x25, matrix products: 122 us -> 117 us  [the longest x15 83.8 us: dot32(): lax.dot_general(left, right, (dims, ((), ())), preferred_element_type=F32)]
  transfers between devices with their start and end apart: 18 -> 14, of which waited for: 12 -> 13; matrix products, arithmetic and copies ran while one was open for 17% -> 23% of each run, Pallas kernels for 0% -> 0%
where the time goes in v1:
time: 769 us; the launch traced here: 762 us
  waiting for transfers between devices  387 us (50%)
  matrix products  125 us (16%)
  blocking collectives  95.4 us (12%)
  local copies, waits for them, and re-layouts  91.7 us (12%)
  other arithmetic  30.7 us (4%)
  between operations  18 us (2%)
  starting transfers between devices  14 us (2%)
    reduce_scatter x1, waiting for transfers between devices, on_device(): lax.psum_scatter(grad_down, 'fsdp', scatter_dimension=0, tiled=True)  99.7 us
    dot_general x15, matrix products, dot32(): lax.dot_general(left, right, (dims, ((), ())), preferred_element_type=F32)  83.8 us
    all_gather x1, waiting for transfers between devices, on_device(): lax.all_gather(lax.dynamic_index_in_dim(expert_out, seq_place, 1, keepdim...  57.3 us
    all_gather x1, waiting for transfers between devices, on_device(): small_full = lax.all_gather(small, 'fsdp', axis=0, tiled=True)  47.3 us
    unnamed x12, waiting for transfers between devices  41.2 us
    psum x1, blocking collectives, on_device(): vectors = lax.psum(vectors, ('fsdp', 'seq'))  38.2 us
    reduce_scatter x1, waiting for transfers between devices, on_device(): lax.psum_scatter(grad_up, 'fsdp', scatter_dimension=0, tiled=True)  27.2 us
    all_gather x1, waiting for transfers between devices, on_device(): lax.all_gather(lax.dynamic_index_in_dim(expert_in, seq_place, 1, keepdims...  26.3 us
  transfers between devices with their start and end apart: 14, of which 13 were waited for; matrix products, arithmetic and copies ran while one was open for 23% of the time, Pallas kernels for 0%

profile of v1, /device:TPU:25, one launch (start us, length us, event | category | flops | bytes accessed | tf_op | source)
XLA Modules:
  0.0 761.7 jit_solution(7695885931911744943)
XLA Ops:
  24.2 47.3 %all-gather.12.cloned.1.call-done = bf16[768,1352]{1,0:T(8,128)(2,1)} async-done(((bf16[96,1352]{1,0:T(8,128)(2,1)}), bf16[768,1352]{1,0:T(8,128)(2,1)}) %all-gather.12.cloned.1.call-update) | async-done | bytes 2076688 | tf_op jit(solution)/shard_map/all_gather | solution.py:85
  78.0 2.9 constant_dynamic-slice_fusion.1
  83.9 12.9 %all-gather.14.cloned.1.call-done = bf16[2,580,768]{2,0,1:T(2,128)(2,1)} async-done(((bf16[2,145,768]{2,0,1:T(2,128)(2,1)}), bf16[2,580,768]{2,0,1:T(2,128)(2,1)}) %all-gather.14.cloned.1.call-update) | async-done | bytes 1781776 | tf_op jit(solution)/shard_map/all_gather | solution.py:109
  96.8 3.4 convolution_convert_fusion.3
  101.5 8.0 %fusion.79 = (f32[2,3,580]{2,1,0:T(4,128)S(1)}, f32[2,3,580,580]{2,3,1,0:T(8,128)}) fusion(pred[580]{0:T(1024)(128)(4,1)S(1)} %lt.70, bf16[3,2,3,580,64]{3,4,2,1,0:T(8,128)(2,1)} %bitcast.168), kind=kOutput, calls=%fused_computation.164 | convolution fusion | flops 266429376 | bytes 9071140 | tf_op jit(solution)/shard_map/sub | solution.py:115
  109.5 4.7 fusion.40
  115.6 3.7 all-to-all-start
  119.4 8.7 %all-to-all-done = bf16[2,580,1,192]{3,0,2,1:T(2,128)(2,1)S(1)} async-done(((bf16[2,580,1,192]{3,0,2,1:T(2,128)(2,1)}), bf16[2,580,1,192]{3,0,2,1:T(2,128)(2,1)S(1)}, u32[]{:S(2)}, u32[]{:S(2)}) %all-to-all-start) | async-done | bytes 445472 | tf_op jit(solution)/shard_map/all_to_all | solution.py:119
  132.6 17.4 %all_to_all.50 = bf16[4,164,768]{2,1,0:T(8,128)(2,1)S(1)} all-to-all(bf16[4,164,768]{2,1,0:T(8,128)(2,1)S(1)} %convolution_convert_fusion.5), channel_id=1, replica_groups=mesh['fsdp'=8,'seq'=4] {'seq'}, dimensions={0} | all-to-all | bytes 2015232 | tf_op jit(solution)/shard_map/all_to_all | solution.py:139
  151.1 26.3 %all-gather.16.cloned.1.call-done = bf16[768,1,3072]{2,0,1:T(8,128)(2,1)} async-done(((bf16[96,1,3072]{2,0,1:T(8,128)(2,1)}), bf16[768,1,3072]{2,0,1:T(8,128)(2,1)}) %all-gather.16.cloned.1.call-update) | async-done | bytes 4718608 | tf_op jit(solution)/shard_map/all_gather | solution.py:90
  177.4 23.4 %multiply_convert_fusion.1 = (bf16[656,3072]{1,0:T(8,128)(2,1)}, f32[656,3072]{1,0:T(8,128)}, f32[656,3072]{1,0:T(8,128)}) fusion(bf16[656,768]{1,0:T(8,128)(2,1)} %reshape.380, bf16[768,1,3072]{2,0,1:T(8,128)(2,1)} %all-gather.16.cloned.1.call-done), kind=kOutput, calls=%fused_computation.8 | convolution fusion | flops 3226386432 | bytes 25878528 | tf_op jit(solution)/shard_map/dot_general | solution.py:40
  200.8 57.3 %all-gather.18.cloned.1.call-done = bf16[3072,1,768]{2,0,1:T(8,128)(2,1)} async-done(((bf16[384,1,768]{2,0,1:T(8,128)(2,1)}), bf16[3072,1,768]{2,0,1:T(8,128)(2,1)}) %all-gather.18.cloned.1.call-update) | async-done | bytes 4718608 | tf_op jit(solution)/shard_map/all_gather | solution.py:93
  258.1 6.8 fusion.32
  266.1 4.0 all-to-all-start.2
  274.7 8.8 %all-to-all-done.2 = bf16[4,164,768]{2,1,0:T(8,128)(2,1)S(1)} async-done(((bf16[4,164,768]{2,1,0:T(8,128)(2,1)}), bf16[4,164,768]{2,1,0:T(8,128)(2,1)S(1)}, u32[]{:S(2)}, u32[]{:S(2)}) %all-to-all-start.2) | async-done | bytes 1007648 | tf_op jit(solution)/shard_map/all_to_all | solution.py:145
  283.5 2.7 multiply_reduce_fusion.2
  288.8 17.5 %all_to_all.51 = bf16[4,164,768]{2,1,0:T(8,128)(2,1)} all-to-all(bf16[4,164,768]{2,1,0:T(8,128)(2,1)S(1)} %fusion.28), channel_id=1, replica_groups=mesh['fsdp'=8,'seq'=4] {'seq'}, dimensions={0} | all-to-all | bytes 2015232 | tf_op jit(solution)/shard_map/all_to_all | solution.py:156
  308.6 10.9 %add_convert_fusion = bf16[656,3072]{1,0:T(8,128)(2,1)S(1)} fusion(f32[656,3072]{1,0:T(8,128)} %get-tuple-element.152, f32[656,3072]{1,0:T(8,128)} %get-tuple-element.161, bf16[656,768]{1,0:T(8,128)(2,1)} %reshape.384, bf16[3072,1,768]{2,0,1:T(8,128)(2,1)} %all-gather.18.cloned.1.call-done), kind=kOutput, calls=%fused_computation.7 | convolution fusion | flops 3123609600 | bytes 25878528 | tf_op jit(solution)/shard_map/dot_general | solution.py:40
  321.4 6.7 fusion.29
  330.5 5.3 all-to-all-start.4
  338.3 11.1 %all-to-all-done.4 = bf16[4,164,768]{2,1,0:T(8,128)(2,1)} async-done(((bf16[4,164,768]{2,1,0:T(8,128)(2,1)}), bf16[4,164,768]{2,1,0:T(8,128)(2,1)}, u32[]{:S(2)}, u32[]{:S(2)}) %all-to-all-start.4) | async-done | bytes 1007648 | tf_op jit(solution)/shard_map/all_to_all | solution.py:163
  351.3 2.6 multiply_reduce_fusion.4
  356.3 8.5 %convolution_convert_fusion.1 = bf16[768,3072]{1,0:T(8,128)(2,1)} fusion(bf16[656,768]{1,0:T(8,128)(2,1)} %reshape.380, bf16[656,3072]{1,0:T(8,128)(2,1)} %copy-done.34), kind=kOutput, calls=%fused_computation.24 | convolution fusion | flops 3097755648 | bytes 9756672 | tf_op jit(solution)/shard_map/dot_general | solution.py:40
  366.0 7.8 %convolution_convert_fusion = bf16[3072,768]{1,0:T(8,128)(2,1)} fusion(bf16[656,3072]{1,0:T(8,128)(2,1)} %get-tuple-element.151, bf16[656,768]{1,0:T(8,128)(2,1)S(1)} %copy-done.14), kind=kOutput, calls=%fused_computation.23 | convolution fusion | flops 3097755648 | bytes 9756672 | tf_op jit(solution)/shard_map/dot_general | solution.py:40
  376.9 12.1 %all_to_all.52 = bf16[2,145,4,192]{3,0,1,2:T(2,128)(2,1)S(1)} all-to-all(bf16[2,145,4,192]{3,0,1,2:T(2,128)(2,1)S(1)} %copy.310), channel_id=1, replica_groups=mesh['fsdp'=8,'seq'=4] {'seq'}, dimensions={2} | all-to-all | bytes 890880 | tf_op jit(solution)/shard_map/all_to_all | solution.py:183
  391.2 9.2 %multiply_reduce_fusion = (f32[2,3,580]{2,1,0:T(4,128)S(1)}, f32[2,3,580,580]{2,3,1,0:T(8,128)}) fusion(f32[2,3,580,580]{2,3,1,0:T(8,128)} %get-tuple-element.158, f32[2,3,580]{2,1,0:T(4,128)S(1)} %copy-done.25, bf16[2,580,3,64]{1,3,2,0:T(8,128)(2,1)S(1)} %reshape.387, bf16[3,2,3,580,64]{3,4,2,1,0:T(8,128)(2,1)} %bitcast.170), kind=kOutput, calls=%fused_computation.3 | convolution fusion | flops 264406912 | bytes 18008640 | tf_op jit(solution)/shard_map/iqhd,ihkd->ihqk/dot_general | solution.py:187
  400.4 9.5 %multiply_convert_fusion = bf16[2,3,580,580]{2,3,1,0:T(8,128)(2,1)} fusion(f32[2,3,580,580]{2,3,1,0:T(8,128)} %get-tuple-element.168, f32[2,3,580]{2,1,0:T(4,128)S(1)} %get-tuple-element.167, f32[2,3,580,580]{2,3,1,0:T(8,128)} %get-tuple-element.158, f32[2,3,580]{2,1,0:T(4,128)S(1)} %copy-done.25), kind=kLoop, calls=%fused_computation.2 | loop fusion | flops 8073600 | bytes 20211840 | tf_op jit(solution)/shard_map/convert_element_type | solution.py:188
  410.0 4.1 fusion.38
  416.1 5.0 fusion.35
  421.4 2.7 copy.315
  424.1 4.7 convert_element_type.213
  428.8 4.8 convolution_convert_fusion.2
  433.6 3.1 reshape.388
  436.7 4.1 copy.316
  440.8 3.0 copy.299
  443.8 3.0 reshape.391
  446.9 3.2 convolution_convert_fusion.6
  452.8 27.2 %reduce-scatter.9.cloned.1.call-done = bf16[96,3072]{1,0:T(8,128)(2,1)} async-done(((bf16[768,3072]{1,0:T(8,128)(2,1)}), bf16[96,3072]{1,0:T(8,128)(2,1)}) %reduce-scatter.9.cloned.1.call-update) | async-done | bytes 589840 | tf_op jit(solution)/shard_map/reduce_scatter | solution.py:167
  480.1 99.7 %reduce-scatter.11.cloned.1.call-done = bf16[384,768]{1,0:T(8,128)(2,1)} async-done(((bf16[3072,768]{1,0:T(8,128)(2,1)}), bf16[384,768]{1,0:T(8,128)(2,1)}) %reduce-scatter.11.cloned.1.call-update) | async-done | bytes 589840 | tf_op jit(solution)/shard_map/reduce_scatter | solution.py:166
  588.7 41.1 %all-reduce.4.cloned.1.call-done = bf16[2,580,768]{2,0,1:T(2,128)(2,1)} async-done(((bf16[2,580,768]{2,0,1:T(2,128)(2,1)}), bf16[2,580,768]{2,0,1:T(2,128)(2,1)}) %all-reduce.4.cloned.1.call-update) | async-done | bytes 1781776
  629.8 5.0 multiply_reduce_fusion.7
  635.1 38.2 %psum.7 = f32[9,768]{1,0:T(8,128)S(1)} all-reduce(f32[9,768]{1,0:T(8,128)S(1)} %concatenate.12), channel_id=1, replica_groups=mesh['fsdp'=8,'seq'=4] {'fsdp','seq'}, use_global_device_ids=true, to_apply=%region_22.23 | all-reduce | flops 6912 | bytes 55296 | tf_op jit(solution)/shard_map/psum | solution.py:210
  681.3 13.3 %reduce-scatter.13.cloned.1.call-done = bf16[96,768]{1,0:T(8,128)(2,1)} async-done(((bf16[768,768]{1,0:T(8,128)(2,1)}), bf16[96,768]{1,0:T(8,128)(2,1)}) %reduce-scatter.13.cloned.1.call-update) | async-done | bytes 147472 | tf_op jit(solution)/shard_map/reduce_scatter | solution.py:203
  694.6 10.2 %all-gather.2 = bf16[384,768]{1,0:T(8,128)(2,1)S(1)} all-gather(bf16[96,768]{1,0:T(8,128)(2,1)} %reduce-scatter.13.cloned.1.call-done), channel_id=4, replica_groups=mesh['fsdp'=8,'seq'=4] {'seq'}, dimensions={0}, use_global_device_ids=true | all-gather | bytes 737280 | tf_op jit(solution)/shard_map/all_gather | solution.py:215
  709.2 13.3 %all-gather.20.cloned.1.call-done = bf16[384,3072]{1,0:T(8,128)(2,1)} async-done(((bf16[96,3072]{1,0:T(8,128)(2,1)}), bf16[384,3072]{1,0:T(8,128)(2,1)}) %all-gather.20.cloned.1.call-update) | async-done | bytes 2359312 | tf_op jit(solution)/shard_map/all_gather | solution.py:221
  722.5 5.8 copy.351
  728.4 19.8 %all-gather.22.cloned.1.call-done = bf16[1536,768]{1,0:T(8,128)(2,1)} async-done(((bf16[384,768]{1,0:T(8,128)(2,1)}), bf16[1536,768]{1,0:T(8,128)(2,1)}) %all-gather.22.cloned.1.call-update) | async-done | bytes 2359312 | tf_op jit(solution)/shard_map/all_gather | solution.py:222
  748.2 5.7 copy.350
  (204 shorter events, 87.4 us)
Async XLA Ops:
  7.2 68.2 %copy-start = (bf16[96,4,3072]{2,1,0:T(4,128)(2,1)S(1)}, bf16[96,4,3072]{2,1,0:T(4,128)(2,1)}, u32[]{:S(2)}) copy-start(bf16[96,4,3072]{2,1,0:T(4,128)(2,1)} %param.28) | copy-start | bytes 7077892
  7.2 16.3 %copy-start.3 = (f32[2,145,768]{2,0,1:T(2,128)S(1)}, f32[2,145,768]{2,0,1:T(2,128)}, u32[]{:S(2)}) copy-start(f32[2,145,768]{2,0,1:T(2,128)} %param.16) | copy-start | bytes 2672644
  7.2 64.3 %all-gather.12.cloned.1.call-start = ((), (), s32[]{:S(2)}) async-start(), calls=%async_computation.10 | async-start | bytes 2433024 | tf_op jit(solution)/shard_map/all_gather | solution.py:85
  22.0 74.8 %all-gather.14.cloned.1.call-start = ((), (), s32[]{:S(2)}) async-start(), calls=%async_computation.11 | async-start | bytes 2227200 | tf_op jit(solution)/shard_map/all_gather | solution.py:109
  23.5 57.4 %copy-start.10 = (f32[2,145]{0,1:T(8,128)}, f32[2,145]{0,1:T(8,128)S(1)}, u32[]{:S(2)}) copy-start(f32[2,145]{0,1:T(8,128)S(1)} %broadcast_multiply_fusion.2) | copy-start | bytes 3484
  24.2 56.7 %copy-start.12 = (f32[2,145]{0,1:T(8,128)}, f32[2,145]{0,1:T(8,128)S(1)}, u32[]{:S(2)}) copy-start(f32[2,145]{0,1:T(8,128)S(1)} %add_rsqrt_fusion) | copy-start | bytes 3484
  73.2 58.4 %copy-start.18 = (f32[768]{0:T(1024)}, f32[768]{0:T(1024)S(1)}, u32[]{:S(2)}) copy-start(f32[768]{0:T(1024)S(1)} %get-tuple-element.134) | copy-start | bytes 9220
  75.3 102.1 %all-gather.16.cloned.1.call-start = ((), (), s32[]{:S(2)}) async-start(), calls=%async_computation.15 | async-start | bytes 5308416 | tf_op jit(solution)/shard_map/all_gather | solution.py:90
  76.6 5.5 copy-start.32
  76.6 6.9 copy-start.30
  76.6 7.0 copy-start.31
  77.7 180.4 %all-gather.18.cloned.1.call-start = ((), (), s32[]{:S(2)}) async-start(), calls=%async_computation.16 | async-start | bytes 5308416 | tf_op jit(solution)/shard_map/all_gather | solution.py:93
  83.9 45.2 %copy-start.5 = (f32[290,768]{1,0:T(8,128)}, f32[290,768]{1,0:T(8,128)S(1)}, u32[]{:S(2)}) copy-start(f32[290,768]{1,0:T(8,128)S(1)} %reshape.374) | copy-start | bytes 2672644
  109.5 4.7 copy-start.24
  115.6 12.5 %all-to-all-start = ((bf16[2,580,1,192]{3,0,2,1:T(2,128)(2,1)}), bf16[2,580,1,192]{3,0,2,1:T(2,128)(2,1)S(1)}, u32[]{:S(2)}, u32[]{:S(2)}) async-start(bf16[2,580,1,192]{3,0,2,1:T(2,128)(2,1)} %copy.302), calls=%async_computation | async-start | bytes 1187840 | tf_op jit(solution)/shard_map/all_to_all | solution.py:119
  129.1 2.6 copy-start.7
  131.4 69.4 %copy-start.20 = (f32[290]{0:T(512)}, f32[290]{0:T(512)S(1)}, u32[]{:S(2)}) copy-start(f32[290]{0:T(512)S(1)} %broadcast_multiply_fusion.5) | copy-start | bytes 3484
  131.6 69.2 %copy-start.22 = (f32[290]{0:T(512)}, f32[290]{0:T(512)S(1)}, u32[]{:S(2)}) copy-start(f32[290]{0:T(512)S(1)} %add_rsqrt_fusion.1) | copy-start | bytes 3484
  264.9 5.2 copy-start.15
  266.1 17.4 %all-to-all-start.2 = ((bf16[4,164,768]{2,1,0:T(8,128)(2,1)}), bf16[4,164,768]{2,1,0:T(8,128)(2,1)S(1)}, u32[]{:S(2)}, u32[]{:S(2)}) async-start(bf16[4,164,768]{2,1,0:T(8,128)(2,1)} %reshape.381), calls=%async_computation.2 | async-start | bytes 2064384 | tf_op jit(solution)/shard_map/all_to_all | solution.py:145
  283.5 2.7 copy-start.9
  319.5 2.0 copy-start.34
  330.5 20.8 %copy-start.19 = (f32[768]{0:T(1024)S(1)}, f32[768]{0:T(1024)}, u32[]{:S(2)}) copy-start(f32[768]{0:T(1024)} %copy-done.18) | copy-start | bytes 9220
  330.5 20.8 %copy-start.21 = (f32[290]{0:T(512)S(1)}, f32[290]{0:T(512)}, u32[]{:S(2)}) copy-start(f32[290]{0:T(512)} %copy-done.20) | copy-start | bytes 3484
  330.5 20.8 %copy-start.23 = (f32[290]{0:T(512)S(1)}, f32[290]{0:T(512)}, u32[]{:S(2)}) copy-start(f32[290]{0:T(512)} %copy-done.22) | copy-start | bytes 3484
  330.5 18.9 %all-to-all-start.4 = ((bf16[4,164,768]{2,1,0:T(8,128)(2,1)}), bf16[4,164,768]{2,1,0:T(8,128)(2,1)}, u32[]{:S(2)}, u32[]{:S(2)}) async-start(bf16[4,164,768]{2,1,0:T(8,128)(2,1)} %reshape.385), calls=%async_computation.4 | async-start | bytes 2064384 | tf_op jit(solution)/shard_map/all_to_all | solution.py:163
  335.8 114.3 %reduce-scatter.7.cloned.1.call-start = ((), (), s32[]{:S(2)}) async-start(), calls=%async_computation.12 | async-start | bytes 1474560 | tf_op jit(solution)/shard_map/reduce_scatter | solution.py:202
  338.3 16.0 %copy-start.26 = (f32[290]{0:T(512)}, f32[290]{0:T(512)S(1)}, u32[]{:S(2)}) copy-start(f32[290]{0:T(512)S(1)} %multiply_reduce_fusion.12) | copy-start | bytes 3484
  349.4 4.9 copy-start.8
  356.2 123.8 %reduce-scatter.9.cloned.1.call-start = ((), (), s32[]{:S(2)}) async-start(), calls=%async_computation.13 | async-start | bytes 5308416 | tf_op jit(solution)/shard_map/reduce_scatter | solution.py:167
  364.8 1.2 copy-start.14
  364.8 214.9 %reduce-scatter.11.cloned.1.call-start = ((), (), s32[]{:S(2)}) async-start(), calls=%async_computation.14 | async-start | bytes 5308416 | tf_op jit(solution)/shard_map/reduce_scatter | solution.py:166
  373.8 17.4 %copy-start.25 = (f32[2,3,580]{2,1,0:T(4,128)S(1)}, f32[2,3,580]{2,1,0:T(4,128)}, u32[]{:S(2)}) copy-start(f32[2,3,580]{2,1,0:T(4,128)} %copy-done.24) | copy-start | bytes 41764
  373.8 255.9 %all-reduce.4.cloned.1.call-start = ((), (), s32[]{:S(2)}) async-start(), calls=%async_computation.20 | async-start | bytes 3563520
  410.0 4.1 copy-start.2
  440.8 253.8 %reduce-scatter.13.cloned.1.call-start = ((), (), s32[]{:S(2)}) async-start(), calls=%async_computation.19 | async-start | bytes 1327104 | tf_op jit(solution)/shard_map/reduce_scatter | solution.py:203
  450.1 129.7 %copy-start.11 = (f32[2,145]{0,1:T(8,128)S(1)}, f32[2,145]{0,1:T(8,128)}, u32[]{:S(2)}) copy-start(f32[2,145]{0,1:T(8,128)} %copy-done.10) | copy-start | bytes 3484
  450.1 131.5 %copy-start.33 = (u32[32]{0:T(128)S(1)}, u32[32]{0:T(128)}, u32[]{:S(2)}) copy-start(u32[32]{0:T(128)} %constant.161) | copy-start | bytes 388
  451.2 137.2 %copy-start.27 = (f32[290]{0:T(512)S(1)}, f32[290]{0:T(512)}, u32[]{:S(2)}) copy-start(f32[290]{0:T(512)} %copy-done.26) | copy-start | bytes 3484
  451.2 178.6 %copy-start.4 = (f32[2,145,768]{2,0,1:T(2,128)S(1)}, f32[2,145,768]{2,0,1:T(2,128)}, u32[]{:S(2)}) copy-start(f32[2,145,768]{2,0,1:T(2,128)} %param.16) | copy-start | bytes 2672644
  451.2 178.6 %copy-start.17 = (f32[768]{0:T(1024)S(1)}, f32[768]{0:T(1024)}, u32[]{:S(2)}) copy-start(f32[768]{0:T(1024)} %copy-done.16) | copy-start | bytes 9220
  452.8 135.9 %copy-start.29 = (f32[768]{0:T(1024)S(1)}, f32[768]{0:T(1024)}, u32[]{:S(2)}) copy-start(f32[768]{0:T(1024)} %get-tuple-element.138) | copy-start | bytes 9220
  452.8 135.9 %copy-start.28 = (f32[768]{0:T(1024)S(1)}, f32[768]{0:T(1024)}, u32[]{:S(2)}) copy-start(f32[768]{0:T(1024)} %get-tuple-element.143) | copy-start | bytes 9220
  452.8 177.0 %copy-start.13 = (f32[2,145]{0,1:T(8,128)S(1)}, f32[2,145]{0,1:T(8,128)}, u32[]{:S(2)}) copy-start(f32[2,145]{0,1:T(8,128)} %copy-done.12) | copy-start | bytes 3484
  452.8 269.7 %all-gather.20.cloned.1.call-start = ((), (), s32[]{:S(2)}) async-start(), calls=%async_computation.17 | async-start | bytes 2949120 | tf_op jit(solution)/shard_map/all_gather | solution.py:221
  480.0 268.2 %all-gather.22.cloned.1.call-start = ((), (), s32[]{:S(2)}) async-start(), calls=%async_computation.18 | async-start | bytes 2949120 | tf_op jit(solution)/shard_map/all_gather | solution.py:222
  585.8 90.7 %copy-start.6 = (f32[290,768]{1,0:T(8,128)S(1)}, f32[290,768]{1,0:T(8,128)}, u32[]{:S(2)}) copy-start(f32[290,768]{1,0:T(8,128)} %copy-done.5) | copy-start | bytes 2672644
  722.5 31.3 %copy-start.1 = (bf16[96,4,3072]{2,1,0:T(4,128)(2,1)S(1)}, bf16[96,4,3072]{2,1,0:T(4,128)(2,1)}, u32[]{:S(2)}) copy-start(bf16[96,4,3072]{2,1,0:T(4,128)(2,1)} %param.28) | copy-start | bytes 7077892
  (1 other events, 0.6 us)
Sparse Core Ops, SparseCore 0:
  22.1 49.3 all-gather.11
  75.4 21.2 all-gather.13
  99.5 77.8 all-gather.15
  180.0 78.0 all-gather.17
  356.3 25.0 reduce-scatter.6
  385.9 94.0 reduce-scatter.8
  484.7 95.0 reduce-scatter.10
  582.3 47.4 all-reduce.3
  633.2 61.3 reduce-scatter.12
  696.0 26.4 all-gather.19
  724.1 24.0 all-gather.21

commit v2 on v1

--- a/solution.py
+++ b/solution.py
@@ -1,6 +1,8 @@
 import jax
 import jax.numpy as jnp
 from jax import lax
+from jax.experimental import pallas as pl
+from jax.experimental.pallas import tpu as pltpu
 from jax.sharding import PartitionSpec as P
 
 HEADS = 12
@@ -40,7 +42,7 @@
     return lax.dot_general(left, right, (dims, ((), ())), preferred_element_type=F32)
 
 
-def on_device(
+def on_device_plain(
     block_in,
     teacher,
     image_counts,
@@ -233,6 +235,779 @@
         owned_vectors[5:].T,
         grad_up_w,
         grad_down_w,
+    )
+
+
+MESH = pl.DeviceIdType.MESH
+LANES = 16
+STATS = 16
+GAIN_ONE, BIAS_ONE, GAIN_TWO, BIAS_TWO = 4, 5, 6, 7
+LOSS_ROW = 8
+
+
+def round_up(value, step):
+    return (value + step - 1) // step * step
+
+
+def flipped(place, bits):
+    low, high = lax.rem(place, 2), place // 2
+    if bits % 2:
+        low = 1 - low
+    if bits // 2:
+        high = 1 - high
+    return high * 2 + low
+
+
+def unit_rows(values_in):
+    centered = values_in - jnp.mean(values_in, axis=1, keepdims=True)
+    variance = jnp.mean(centered * centered, axis=1, keepdims=True)
+    root = lax.rsqrt(variance + NORM_EPS)
+    return centered * root, root
+
+
+def norm_back(grad_out, unit, root, gain_row):
+    scaled = grad_out * gain_row
+    return root * (
+        scaled
+        - jnp.mean(scaled, axis=1, keepdims=True)
+        - unit * jnp.mean(scaled * unit, axis=1, keepdims=True)
+    )
+
+
+def hi_lo(values_in):
+    high = values_in.astype(BF16)
+    return high, (values_in - high.astype(F32)).astype(BF16)
+
+
+def block_kernel(
+    sizes,
+    x_in,
+    teacher_in,
+    route_rows,
+    route_cols,
+    vec_in,
+    attn_in,
+    up_in,
+    down_in,
+    block_out,
+    input_grad,
+    stats_out,
+    attn_all,
+    up_all,
+    down_all,
+    zrecv_down,
+    zrecv_up,
+    zrecv_attn,
+    vec_all,
+    vecs,
+    attn_w,
+    out_w,
+    up_w,
+    down_w,
+    low_all,
+    qkv_s,
+    lse_s,
+    ctx_s,
+    ctx_rows,
+    middle,
+    misfit,
+    low_two,
+    select,
+    select_t,
+    hits,
+    weights,
+    send_s,
+    arrived,
+    ret_r,
+    back_r,
+    dret_r,
+    turned,
+    act,
+    slope,
+    grad_down,
+    yrecv_down,
+    yrecv_up,
+    dctx_s,
+    half_recv,
+    yrecv_attn,
+    part_s,
+    part_r,
+    stats,
+    stats_r,
+    send_sem,
+    recv_sem,
+    local_sem,
+):
+    images, piece, padded, cap, features, cols, ffn, in_rows, out_rows = sizes
+    rows = images * padded
+    slots = 4 * padded
+    half_cols = features // 2
+    wide = ffn // 6
+    f = lax.axis_index("fsdp")
+    s = lax.axis_index("seq")
+    z, y = f // 2, lax.rem(f, 2)
+    inv_root = HD ** (-0.5)
+    same = [flipped(z, k) * 2 + y for k in range(4)]
+    other = [flipped(z, k) * 2 + (1 - y) for k in range(4)]
+    near = [flipped(s, r) for r in range(4)]
+    counter = [0, 0]
+    pending = []
+
+    def send(src, dst, group, seq):
+        i = counter[0]
+        counter[0] += 1
+        copy = pltpu.make_async_remote_copy(
+            src_ref=src,
+            dst_ref=dst,
+            send_sem=send_sem.at[i],
+            recv_sem=recv_sem.at[i],
+            device_id=(group, seq),
+            device_id_type=MESH,
+        )
+        copy.start()
+        pending.append(copy)
+        return copy
+
+    def done_sending(copy):
+        pending[:] = [other_copy for other_copy in pending if other_copy is not copy]
+        copy.wait_send()
+
+    def local(src, dst):
+        i = counter[1]
+        counter[1] += 1
+        copy = pltpu.make_async_copy(src, dst, local_sem.at[i])
+        copy.start()
+        return copy
+
+    barrier = pltpu.get_barrier_semaphore()
+    for g in same[1:] + other:
+        pl.semaphore_signal(barrier, inc=1, device_id=(g, s), device_id_type=MESH)
+    for q in near[1:]:
+        pl.semaphore_signal(barrier, inc=1, device_id=(f, q), device_id_type=MESH)
+    pl.semaphore_wait(barrier, 10)
+
+    vec_copies = [send(vec_in, vec_all.at[f], g, s) for g in same[1:] + other]
+    vec_all[f] = vec_in[...]
+
+    def spot(ref, n, g):
+        return ref.at[pl.ds(pl.multiple_of(g * n, n), n), :]
+
+    def gather_start(src, dst, n):
+        along_z = [None] + [send(src, spot(dst, n, f), same[k], s) for k in (1, 2, 3)]
+        across = [send(src, spot(dst, n, f), other[0], s)]
+        return along_z, across, local(src, spot(dst, n, f))
+
+    def gather_pass(flow, dst, n, k):
+        along_z, across, _ = flow
+        along_z[k].wait_recv()
+        across.append(send(spot(dst, n, same[k]), spot(dst, n, same[k]), other[0], s))
+
+    def gather_end(flow):
+        for copy in flow[1]:
+            copy.wait_recv()
+        flow[2].wait()
+
+    attn_flow = gather_start(attn_in, attn_w, in_rows)
+
+    own_near = near
+
+    def near_of(shape, axis):
+        at = lax.broadcasted_iota(jnp.int32, shape, axis)
+        named = jnp.full(shape, -1, jnp.int32)
+        for r in range(4):
+            named = jnp.where(at == r, own_near[r], named)
+        return named
+
+    named = near_of((rows, LANES), 1)
+    hit = ((route_rows[:, 0:1] == named) & (route_rows[:, 2:3] == 1)) | (
+        (route_rows[:, 1:2] == named) & (route_rows[:, 3:4] == 1)
+    )
+    hit_f = jnp.where(hit, 1.0, 0.0)
+    before = (
+        lax.broadcasted_iota(jnp.int32, (rows, rows), 0) > lax.broadcasted_iota(jnp.int32, (rows, rows), 1)
+    )
+    before = jnp.where(before, 1.0, 0.0).astype(BF16)
+    place = dot32(before, hit_f.astype(BF16), ((1,), (0,)))
+    place = jnp.where(hit, place, -1.0)
+    hits[...] = hit_f
+    named_t = near_of((LANES, rows), 0)
+    hit_t = ((route_cols[0:1, :] == named_t) & (route_cols[2:3, :] == 1)) | (
+        (route_cols[1:2, :] == named_t) & (route_cols[3:4, :] == 1)
+    )
+    hit_tf = jnp.where(hit_t, 1.0, 0.0).astype(BF16)
+    place_t = dot32(hit_tf, before, ((1,), (1,)))
+    place_t = jnp.where(hit_t, place_t, -1.0)
+    slot_down = lax.broadcasted_iota(jnp.int32, (cap, rows), 0).astype(F32)
+    slot_along = lax.broadcasted_iota(jnp.int32, (rows, cap), 1).astype(F32)
+    for r in range(4):
+        select[r] = jnp.where(place_t[r : r + 1, :] == slot_down, 1.0, 0.0).astype(BF16)
+        select_t[r] = jnp.where(place[:, r : r + 1] == slot_along, 1.0, 0.0).astype(BF16)
+
+    for copy in vec_copies:
+        copy.wait_recv()
+    at_row = lax.broadcasted_iota(jnp.int32, (128, features), 0)
+    at_col = lax.broadcasted_iota(jnp.int32, (128, features), 1)
+    total = jnp.zeros((STATS, features), F32)
+    for g in range(8):
+        spread = jnp.where((at_col - g * in_rows == at_row) & (at_row < in_rows), 1.0, 0.0).astype(BF16)
+        total = total + dot32(vec_all[g], spread, ((1,), (0,)))
+    vecs[...] = total
+
+    low_all[s] = jnp.zeros((rows, features), BF16)
+    for i in range(images):
+        unit, _ = unit_rows(x_in[i])
+        low_all[s, i * padded : i * padded + piece, :] = (
+            unit * vecs[GAIN_ONE : GAIN_ONE + 1, :] + vecs[BIAS_ONE : BIAS_ONE + 1, :]
+        ).astype(BF16)
+    low_x = send(low_all.at[s], low_all.at[s], f, near[2])
+    low_c = send(low_all.at[s], low_all.at[s], f, near[1])
+
+    for k in (1, 2, 3):
+        gather_pass(attn_flow, attn_w, in_rows, k)
+    up_flow = gather_start(up_in, up_w, in_rows)
+    low_x.wait_recv()
+    low_d = send(low_all.at[near[2]], low_all.at[near[2]], f, near[1])
+    gather_end(attn_flow)
+    mine = lax.rem(s, 2)
+    here = pl.ds(pl.multiple_of(mine * half_cols, half_cols), half_cols)
+    there = pl.ds(pl.multiple_of((1 - mine) * half_cols, half_cols), half_cols)
+    out_half = send(attn_w.at[:, pl.ds(0, half_cols)], out_w.at[:, here], f, near[1])
+    out_w[:, here] = attn_w[:, 0:half_cols]
+
+    def project(j):
+        found = dot32(low_all[j], attn_w[:, half_cols:], ((1,), (0,))).astype(BF16)
+        for i in range(images):
+            qkv_s[i, pl.ds(pl.multiple_of(j * padded, padded), padded), :] = found[
+                i * padded : (i + 1) * padded, :
+            ]
+
+    project(s)
+    low_c.wait_recv()
+    project(near[1])
+    project(near[2])
+    low_d.wait_recv()
+    project(near[3])
+
+    key_at = lax.broadcasted_iota(jnp.int32, (slots, 1), 0)
+    key_piece = jnp.zeros((slots, 1), jnp.int32)
+    for j in range(1, 4):
+        key_piece = key_piece + jnp.where(key_at >= j * padded, 1, 0)
+    key_len = SEQ_LEN // 4 + jnp.where(key_piece < SEQ_LEN % 4, 1, 0)
+    key_ok = key_at - key_piece * padded < key_len
+
+    def heads_of(ref, i, kind, h):
+        return ref[i, :, kind * cols + h * HD : kind * cols + (h + 1) * HD]
+
+    def scores_of(i, h):
+        found = dot32(heads_of(qkv_s, i, 1, h), heads_of(qkv_s, i, 0, h), ((1,), (1,))) * inv_root
+        return jnp.where(key_ok, found, -1e30)
+
+    gather_pass(up_flow, up_w, in_rows, 1)
+    down_flow = gather_start(down_in, down_w, out_rows)
+
+    @pl.loop(0, images)
+    def _(i):
+        found = []
+        for h in range(cols // HD):
+            scores = scores_of(i, h)
+            highest = jnp.max(scores, axis=0, keepdims=True)
+            raised = jnp.exp(scores - highest)
+            total = jnp.sum(raised, axis=0, keepdims=True)
+            shares = (raised * (1.0 / total)).astype(BF16)
+            lse_s[i, h : h + 1, :] = highest + jnp.log(total)
+            found.append(dot32(heads_of(qkv_s, i, 2, h), shares, ((0,), (0,))))
+        ctx_s[i] = jnp.concatenate(found, axis=0).T.astype(BF16)
+
+    def piece_rows(ref, j):
+        return ref.at[:, pl.ds(pl.multiple_of(j * padded, padded), padded), :]
+
+    ctx_copies = [send(piece_rows(ctx_s, near[r]), ctx_rows.at[s], f, near[r]) for r in (2, 3, 1)]
+    ctx_rows[s] = ctx_s[:, pl.ds(pl.multiple_of(s * padded, padded), padded), :]
+    for k in (2, 3):
+        gather_pass(up_flow, up_w, in_rows, k)
+    out_half.wait_recv()
+    for copy in ctx_copies:
+        copy.wait_recv()
+        done_sending(copy)
+
+    attended = jnp.zeros((rows, features), F32)
+    for j in range(4):
+        attended = attended + dot32(
+            ctx_rows[j].reshape(rows, cols), out_w[j * cols : (j + 1) * cols, :], ((1,), (0,))
+        )
+    middle[...] = attended
+    for i in range(images):
+        at = slice(i * padded, i * padded + piece)
+        middle[at, :] = middle[at, :] + x_in[i]
+    unit, _ = unit_rows(middle[...])
+    low_two[...] = (unit * vecs[GAIN_TWO : GAIN_TWO + 1, :] + vecs[BIAS_TWO : BIAS_TWO + 1, :]).astype(BF16)
+    router = vecs[...].astype(BF16)
+
+    def probs_of():
+        logits = dot32(low_two[...], router, ((1,), (1,)))
+        real = lax.broadcasted_iota(jnp.int32, (rows, LANES), 1) < EXPERTS
+        logits = jnp.where(real, logits, -1e30)
+        raised = jnp.exp(logits - jnp.max(logits, axis=1, keepdims=True))
+        return raised / jnp.sum(raised, axis=1, keepdims=True)
+
+    disp_copies = []
+    for r in (2, 3, 1, 0):
+        found = dot32(select[r], low_two[...], ((1,), (0,))).astype(BF16)
+        if r:
+            send_s[r - 1] = found
+            disp_copies.append(send(send_s.at[r - 1], arrived.at[r], f, near[r]))
+        else:
+            arrived[0] = found
+    probs = probs_of()
+    lane = lax.broadcasted_iota(jnp.int32, (rows, LANES), 1)
+    chosen = jnp.zeros((rows, LANES), F32)
+    for r in range(4):
+        value = jnp.sum(jnp.where(lane == near[r], probs, 0.0), axis=1, keepdims=True)
+        chosen = jnp.where(lane == r, value, chosen)
+    weights[...] = chosen * hits[...]
+
+    gather_end(up_flow)
+    gather_pass(down_flow, down_w, out_rows, 1)
+
+    def expert_up(half):
+        given = arrived[2 * half : 2 * half + 2].reshape(2 * cap, features)
+
+        @pl.loop(0, 6)
+        def _(t):
+            tile = pl.ds(pl.multiple_of(t * wide, wide), wide)
+            hidden = dot32(given, up_w[:, tile], ((1,), (0,)))
+            phi = 0.5 * (1.0 + lax.erf(hidden * (2.0**-0.5)))
+            at = slice(2 * half * cap, 2 * (half + 1) * cap)
+            act[at, tile] = (hidden * phi).astype(BF16)
+            slope[at, tile] = (phi + hidden * jnp.exp(-0.5 * hidden * hidden) * 0.3989422804014327).astype(BF16)
+
+    disp_copies[2].wait_recv()
+    expert_up(0)
+    disp_copies[0].wait_recv()
+    disp_copies[1].wait_recv()
+    expert_up(1)
+    for k in (2, 3):
+        gather_pass(down_flow, down_w, out_rows, k)
+    for copy in disp_copies:
+        done_sending(copy)
+    gather_end(down_flow)
+
+    def to_rows(left, right, dims, half, dst):
+        at = slice(2 * half * cap, 2 * (half + 1) * cap)
+        found = dot32(left[at, :], right[...], dims).astype(BF16)
+        out = []
+        for r in (2 * half, 2 * half + 1):
+            part = found[(r - 2 * half) * cap : (r - 2 * half + 1) * cap, :]
+            if r:
+                send_s[r - 1] = part
+                out.append(send(send_s.at[r - 1], dst.at[r], f, near[r]))
+            else:
+                dst[0] = part
+        return out
+
+    ret_copies = to_rows(act, down_w, ((1,), (0,)), 1, ret_r)
+    ret_copies += to_rows(act, down_w, ((1,), (0,)), 0, ret_r)
+    for i in range(images):
+        at = slice(i * padded, i * padded + piece)
+        misfit[at, :] = teacher_in[i]
+        misfit[i * padded + piece : (i + 1) * padded, :] = jnp.zeros((padded - piece, features), F32)
+    for copy in ret_copies:
+        copy.wait_recv()
+
+    found = middle[...]
+    for r in range(4):
+        found = found + weights[:, r : r + 1] * dot32(select_t[r], ret_r[r], ((1,), (0,)))
+    for i in range(images):
+        block_out[i] = found[i * padded : i * padded + piece, :]
+    token_ok = route_rows[:, 4:5].astype(F32)
+    wrong = (found - misfit[...]) * token_ok
+    misfit[...] = wrong
+    for copy in ret_copies:
+        done_sending(copy)
+    dret_copies = []
+    for r in (2, 3, 1, 0):
+        pair = (weights[:, r : r + 1] * misfit[...]).astype(BF16)
+        part = dot32(select[r], pair, ((1,), (0,))).astype(BF16)
+        if r:
+            send_s[r - 1] = part
+            dret_copies.append(send(send_s.at[r - 1], dret_r.at[r], f, near[r]))
+        else:
+            dret_r[0] = part
+    stats[...] = jnp.zeros_like(stats)
+    stats[LOSS_ROW : LOSS_ROW + 1, :] = jnp.sum(wrong * wrong, axis=0, keepdims=True)
+    probs = probs_of()
+    prob_grad = jnp.zeros((rows, LANES), F32)
+    for r in range(4):
+        picked = dot32(select_t[r], ret_r[r], ((1,), (0,)))
+        value = jnp.sum(picked * misfit[...], axis=1, keepdims=True) * hits[:, r : r + 1]
+        prob_grad = jnp.where(lane == near[r], value, prob_grad)
+    logit_grad = probs * (prob_grad - jnp.sum(probs * prob_grad, axis=1, keepdims=True))
+    high, low = hi_lo(logit_grad)
+    router_grad = dot32(high, low_two[...], ((0,), (0,))) + dot32(low, low_two[...], ((0,), (0,)))
+    stats[0:EXPERTS, :] = router_grad[0:EXPERTS, :]
+    for copy in dret_copies:
+        copy.wait_recv()
+
+    given = dret_r[...].reshape(4 * cap, features)
+    turned[...] = given.T
+
+    @pl.loop(0, 8)
+    def _(g):
+        grad_down[g] = dot32(
+            turned[...], act[:, pl.ds(pl.multiple_of(g * out_rows, out_rows), out_rows)], ((1,), (0,))
+        ).astype(BF16)
+
+    def down_block(g):
+        return grad_down.at[g]
+
+    def up_block(g):
+        return spot(up_w, in_rows, g)
+
+    def attn_block(g):
+        return spot(attn_w, in_rows, g)
+
+    def sum_start(block, yrecv):
+        return {k: send(block(other[k]), yrecv.at[k], other[0], s) for k in (3, 2, 1, 0)}
+
+    def sum_pass(flow, block, yrecv, zrecv, k):
+        flow[k].wait_recv()
+        ref = block(same[k])
+        ref[...] = (ref[...].astype(F32) + yrecv[k].astype(F32)).astype(BF16)
+        if k:
+            flow["z%d" % k] = send(ref, zrecv.at[k - 1], same[k], s)
+
+    def sum_end(flow, block, yrecv, zrecv, dst):
+        ref = block(f)
+        loads = []
+        for k in (1, 2, 3):
+            flow["z%d" % k].wait_recv()
+            loads.append(local(zrecv.at[k - 1], yrecv.at[k]))
+        for copy in loads:
+            copy.wait()
+        total = ref[...].astype(F32)
+        for k in (1, 2, 3):
+            total = total + yrecv[k].astype(F32)
+        ref[...] = total.astype(BF16)
+        to_x = send(ref, dst.at[s], f, near[2])
+        to_c = send(ref, dst.at[s], f, near[1])
+        return to_x, to_c, local(ref, dst.at[s])
+
+    def share_pass(flow, dst):
+        flow[0].wait_recv()
+        return send(dst.at[near[2]], dst.at[near[2]], f, near[1])
+
+    down_sum = sum_start(down_block, yrecv_down)
+
+    @pl.loop(0, 6)
+    def _(t):
+        tile = pl.ds(pl.multiple_of(t * wide, wide), wide)
+        found = dot32(dret_r[...].reshape(4 * cap, features), down_w[tile, :], ((1,), (1,)))
+        act[:, tile] = (found * slope[:, tile].astype(F32)).astype(BF16)
+
+    for copy in dret_copies:
+        done_sending(copy)
+    back_copies = to_rows(act, up_w, ((1,), (1,)), 1, back_r)
+    back_copies += to_rows(act, up_w, ((1,), (1,)), 0, back_r)
+    sum_pass(down_sum, down_block, yrecv_down, zrecv_down, 3)
+    for copy in up_flow[0][1:] + up_flow[1]:
+        done_sending(copy)
+    given = arrived[...].reshape(4 * cap, features)
+    turned[...] = given.T
+
+    @pl.loop(0, 6)
+    def _(t):
+        tile = pl.ds(pl.multiple_of(t * wide, wide), wide)
+        up_w[:, tile] = dot32(turned[...], act[:, tile], ((1,), (0,))).astype(BF16)
+
+    up_sum = sum_start(up_block, yrecv_up)
+    sum_pass(down_sum, down_block, yrecv_down, zrecv_down, 2)
+
+    normed_grad = dot32(high, router, ((1,), (0,))) + dot32(low, router, ((1,), (0,)))
+    for copy in back_copies:
+        copy.wait_recv()
+    for r in range(4):
+        normed_grad = normed_grad + dot32(select_t[r], back_r[r], ((1,), (0,)))
+    unit, root = unit_rows(middle[...])
+    stats[GAIN_TWO : GAIN_TWO + 1, :] = jnp.sum(normed_grad * unit, axis=0, keepdims=True)
+    stats[BIAS_TWO : BIAS_TWO + 1, :] = jnp.sum(normed_grad, axis=0, keepdims=True)
+    middle_grad = misfit[...] + norm_back(normed_grad, unit, root, vecs[GAIN_TWO : GAIN_TWO + 1, :])
+    middle[...] = middle_grad
+    low_two[...] = middle_grad.astype(BF16)
+
+    dctx_copies = []
+    for r in (2, 3, 1, 0):
+        block = out_w[pl.ds(pl.multiple_of(near[r] * cols, cols), cols), :]
+        found = dot32(low_two[...], block, ((1,), (1,))).astype(BF16).reshape(images, padded, cols)
+        if r:
+            dctx_s[r - 1] = found
+            dctx_copies.append(send(dctx_s.at[r - 1], piece_rows(ctx_s, s), f, near[r]))
+        else:
+            ctx_s[:, pl.ds(pl.multiple_of(s * padded, padded), padded), :] = found
+    done_sending(out_half)
+    for j in range(4):
+        out_w[j * cols : (j + 1) * cols, :] = dot32(
+            ctx_rows[j].reshape(rows, cols), low_two[...], ((0,), (0,))
+        ).astype(BF16)
+    half_copy = send(out_w.at[:, there], half_recv, f, near[1])
+    sum_pass(down_sum, down_block, yrecv_down, zrecv_down, 1)
+    for copy in dctx_copies:
+        copy.wait_recv()
+
+    @pl.loop(0, images)
+    def _(i):
+        found = [[], [], []]
+        for h in range(cols // HD):
+            shares = jnp.exp(scores_of(i, h) - lse_s[i, h : h + 1, :])
+            given = ctx_s[i, :, h * HD : (h + 1) * HD]
+            found[2].append(dot32(shares.astype(BF16), given, ((1,), (0,))))
+            share_grad = dot32(heads_of(qkv_s, i, 2, h), given, ((1,), (1,)))
+            across = jnp.sum(shares * share_grad, axis=0, keepdims=True)
+            score_grad = (shares * (share_grad - across)).astype(BF16)
+            found[1].append(dot32(score_grad, heads_of(qkv_s, i, 0, h), ((1,), (0,))) * inv_root)
+            query_t = dot32(heads_of(qkv_s, i, 1, h), score_grad, ((0,), (0,))) * inv_root
+            found[0].append(query_t.T)
+        for kind in range(3):
+            whole = jnp.concatenate(found[kind], axis=1).astype(BF16)
+            found[kind] = whole
+        qkv_s[i] = jnp.concatenate(found, axis=1)
+
+    sum_pass(down_sum, down_block, yrecv_down, zrecv_down, 0)
+
+    def dqkv_rows(j):
+        return qkv_s[:, pl.ds(pl.multiple_of(j * padded, padded), padded), :].reshape(rows, 3 * cols)
+
+    def low_part(j):
+        return dot32(dqkv_rows(j), attn_w[:, half_cols:], ((1,), (1,)))
+
+    part_s[0] = low_part(near[3]).astype(BF16)
+    part_c = send(part_s.at[0], part_r.at[0], f, near[1])
+    part_s[1] = low_part(near[1]).astype(BF16)
+    part_d = send(part_s.at[1], part_r.at[1], f, near[1])
+    for_x = low_part(near[2])
+    part_c.wait_recv()
+    part_s[2] = (for_x + part_r[0].astype(F32)).astype(BF16)
+    part_x = send(part_s.at[2], part_r.at[2], f, near[2])
+    sum_pass(up_sum, up_block, yrecv_up, zrecv_up, 3)
+    down_share = sum_end(down_sum, down_block, yrecv_down, zrecv_down, down_all)
+
+    misfit[...] = low_part(s)
+
+    for copy in attn_flow[1]:
+        done_sending(copy)
+    qkv_grad = jnp.zeros((features, 3 * cols), F32)
+    for i in range(images):
+        given = low_all[:, i * padded : (i + 1) * padded, :].reshape(4 * padded, features)
+        qkv_grad = qkv_grad + dot32(given, qkv_s[i], ((0,), (0,)))
+    attn_w[:, half_cols:] = qkv_grad.astype(BF16)
+    half_copy.wait_recv()
+    attn_w[:, 0:half_cols] = (out_w[:, here].astype(F32) + half_recv[...].astype(F32)).astype(BF16)
+    attn_sum = sum_start(attn_block, yrecv_attn)
+    sum_pass(up_sum, up_block, yrecv_up, zrecv_up, 2)
+
+    part_d.wait_recv()
+    low_grad = misfit[...] + part_r[1].astype(F32)
+    part_x.wait_recv()
+    low_grad = low_grad + part_r[2].astype(F32)
+    misfit[...] = low_grad
+    stats[BIAS_ONE : BIAS_ONE + 1, :] = jnp.sum(low_grad, axis=0, keepdims=True)
+    gain_grad = jnp.zeros((1, features), F32)
+    for i in range(images):
+        at = slice(i * padded, i * padded + piece)
+        unit, root = unit_rows(x_in[i])
+        gain_grad = gain_grad + jnp.sum(misfit[at, :] * unit, axis=0, keepdims=True)
+        input_grad[i] = middle[at, :] + norm_back(misfit[at, :], unit, root, vecs[GAIN_ONE : GAIN_ONE + 1, :])
+    stats[GAIN_ONE : GAIN_ONE + 1, :] = gain_grad
+
+    seq_copies = [send(stats, stats_r.at[r - 1], f, near[r]) for r in (1, 2, 3)]
+    down_last = share_pass(down_share, down_all)
+    for copy in seq_copies:
+        copy.wait_recv()
+        done_sending(copy)
+    stats[...] = stats[...] + stats_r[0] + stats_r[1] + stats_r[2]
+    y_copy = send(stats, stats_r.at[3], other[0], s)
+    sum_pass(up_sum, up_block, yrecv_up, zrecv_up, 1)
+    y_copy.wait_recv()
+    done_sending(y_copy)
+    stats[...] = stats[...] + stats_r[3]
+    z_copies = [send(stats, stats_r.at[3 + k], same[k], s) for k in (1, 2, 3)]
+    sum_pass(up_sum, up_block, yrecv_up, zrecv_up, 0)
+    for copy in z_copies:
+        copy.wait_recv()
+    stats_out[...] = stats[...] + stats_r[4] + stats_r[5] + stats_r[6]
+
+    up_share = sum_end(up_sum, up_block, yrecv_up, zrecv_up, up_all)
+    for k in (3, 2, 1, 0):
+        sum_pass(attn_sum, attn_block, yrecv_attn, zrecv_attn, k)
+    up_last = share_pass(up_share, up_all)
+    attn_share = sum_end(attn_sum, attn_block, yrecv_attn, zrecv_attn, attn_all)
+    attn_last = share_pass(attn_share, attn_all)
+    for share, last in ((down_share, down_last), (up_share, up_last), (attn_share, attn_last)):
+        share[1].wait_recv()
+        share[2].wait()
+        last.wait_recv()
+    for copy in list(pending):
+        done_sending(copy)
+
+
+def run_block(sizes, operands):
+    images, piece, padded, cap, features, cols, ffn, in_rows, out_rows = sizes
+    rows = images * padded
+    half_cols = features // 2
+    pack = half_cols + 3 * cols
+    shape = jax.ShapeDtypeStruct
+    vmem = pl.BlockSpec(memory_space=pltpu.VMEM)
+    hbm = pl.BlockSpec(memory_space=pl.ANY)
+    scratch = [
+        pltpu.VMEM((8, STATS, 128), BF16),
+        pltpu.VMEM((STATS, features), F32),
+        pltpu.VMEM((8 * in_rows, pack), BF16),
+        pltpu.VMEM((features, features), BF16),
+        pltpu.VMEM((features, ffn), BF16),
+        pltpu.VMEM((ffn, features), BF16),
+        pltpu.VMEM((4, rows, features), BF16),
+        pltpu.VMEM((images, 4 * padded, 3 * cols), BF16),
+        pltpu.VMEM((images, 8, 4 * padded), F32),
+        pltpu.VMEM((images, 4 * padded, cols), BF16),
+        pltpu.VMEM((4, images, padded, cols), BF16),
+        pltpu.VMEM((rows, features), F32),
+        pltpu.VMEM((rows, features), F32),
+        pltpu.VMEM((rows, features), BF16),
+        pltpu.VMEM((4, cap, rows), BF16),
+        pltpu.VMEM((4, rows, cap), BF16),
+        pltpu.VMEM((rows, LANES), F32),
+        pltpu.VMEM((rows, LANES), F32),
+        pltpu.VMEM((3, cap, features), BF16),
+        pltpu.VMEM((4, cap, features), BF16),
+        pltpu.VMEM((4, cap, features), BF16),
+        pltpu.VMEM((4, cap, features), BF16),
+        pltpu.VMEM((4, cap, features), BF16),
+        pltpu.VMEM((features, 4 * cap), BF16),
+        pltpu.VMEM((4 * cap, ffn), BF16),
+        pltpu.VMEM((4 * cap, ffn), BF16),
+        pltpu.VMEM((8, features, out_rows), BF16),
+        pltpu.VMEM((4, features, out_rows), BF16),
+        pltpu.VMEM((4, in_rows, ffn), BF16),
+        pltpu.VMEM((3, images, padded, cols), BF16),
+        pltpu.VMEM((features, half_cols), BF16),
+        pltpu.VMEM((4, in_rows, pack), BF16),
+        pltpu.VMEM((3, rows, features), BF16),
+        pltpu.VMEM((3, rows, features), BF16),
+        pltpu.VMEM((STATS, features), F32),
+        pltpu.VMEM((7, STATS, features), F32),
+        pltpu.SemaphoreType.DMA((112,)),
+        pltpu.SemaphoreType.DMA((112,)),
+        pltpu.SemaphoreType.DMA((16,)),
+    ]
+    return pl.pallas_call(
+        lambda *refs: block_kernel(sizes, *refs),
+        out_shape=(
+            shape((images, piece, features), F32),
+            shape((images, piece, features), F32),
+            shape((STATS, features), F32),
+            shape((4, in_rows, pack), BF16),
+            shape((4, in_rows, ffn), BF16),
+            shape((4, features, out_rows), BF16),
+            shape((3, features, out_rows), BF16),
+            shape((3, in_rows, ffn), BF16),
+            shape((3, in_rows, pack), BF16),
+        ),
+        in_specs=[vmem, vmem, vmem, vmem, vmem, hbm, hbm, hbm],
+        out_specs=(vmem, vmem, vmem, hbm, hbm, hbm, hbm, hbm, hbm),
+        scratch_shapes=scratch,
+        compiler_params=pltpu.CompilerParams(
+            collective_id=0, has_side_effects=True, vmem_limit_bytes=63_000_000
+        ),
+        name="block",
+    )(*operands)
+
+
+def on_device(
+    block_in,
+    teacher,
+    image_counts,
+    expert_ids,
+    pair_keep,
+    norm1_gain,
+    norm1_bias,
+    qkv_weight,
+    out_weight,
+    norm2_gain,
+    norm2_bias,
+    router_weight,
+    expert_in,
+    expert_out,
+):
+    arguments = (
+        block_in, teacher, image_counts, expert_ids, pair_keep, norm1_gain, norm1_bias, qkv_weight,
+        out_weight, norm2_gain, norm2_bias, router_weight, expert_in, expert_out,
+    )
+    images, piece_len, features = block_in.shape
+    pieces = lax.axis_size("seq")
+    groups = lax.axis_size("fsdp")
+    in_rows, out_rows, ffn = expert_in.shape[0], expert_out.shape[0], expert_in.shape[2]
+    if pieces != EXPERTS or groups != 8 or in_rows % 16 or in_rows > 128 or out_rows % 128:
+        return on_device_plain(*arguments)
+    s = lax.axis_index("seq")
+    f = lax.axis_index("fsdp")
+    rows = images * piece_len
+    cols = HEADS // pieces * HD
+    padded = round_up(piece_len, 16)
+    cap = round_up(rows * TOPK * 9 // (EXPERTS * 8) + 1, 16)
+    half_cols = features // 2
+
+    own_len = SEQ_LEN // pieces + (s < SEQ_LEN % pieces).astype(jnp.int32)
+    count = jnp.sum(
+        jnp.where(jnp.arange(image_counts.shape[0], dtype=jnp.int32) == f, image_counts, 0)
+    )
+    token_ok = (jnp.arange(images)[:, None] < count) & (jnp.arange(piece_len)[None, :] < own_len)
+    usable = ((pair_keep[0] == 1) & token_ok[:, :, None]).astype(jnp.int32)
+    route = jnp.concatenate([expert_ids[0], usable, token_ok[:, :, None].astype(jnp.int32)], axis=2)
+    route = jnp.pad(route, ((0, 0), (0, padded - piece_len), (0, 3))).reshape(images * padded, 8)
+
+    vec = jnp.concatenate(
+        [router_weight.T, jnp.stack([norm1_gain, norm1_bias, norm2_gain, norm2_bias], axis=0)], axis=0
+    )
+    vec = jnp.pad(vec, ((0, STATS - 8), (0, 128 - in_rows)))
+    attn_shard = jnp.concatenate(
+        [
+            lax.dynamic_slice_in_dim(out_weight, lax.rem(s, 2) * half_cols, half_cols, axis=1),
+            lax.dynamic_index_in_dim(
+                qkv_weight.reshape(in_rows, 3, pieces, cols), s, 2, keepdims=False
+            ).reshape(in_rows, 3 * cols),
+        ],
+        axis=1,
+    )
+    up_shard = lax.dynamic_index_in_dim(expert_in, s, 1, keepdims=False)
+    down_shard = lax.dynamic_index_in_dim(expert_out, s, 1, keepdims=False)
+    sizes = (images, piece_len, padded, cap, features, cols, ffn, in_rows, out_rows)
+    block_out, input_grad, stats, attn_all, up_all, down_all, *_ = run_block(
+        sizes, (block_in, teacher, route, route.T, vec, attn_shard, up_shard, down_shard)
+    )
+    mean_loss = jnp.sum(stats[LOSS_ROW]) / (
+        (jnp.sum(image_counts, dtype=jnp.int32) * SEQ_LEN).astype(F32) * features
+    )
+    own = lax.dynamic_slice_in_dim(stats, f * in_rows, in_rows, axis=1)
+    grad_qkv = (
+        attn_all[:, :, half_cols:].reshape(pieces, in_rows, 3, cols).transpose(1, 2, 0, 3)
+        .reshape(in_rows, 3 * features).astype(F32)
+    )
+    halves = attn_all[:, :, :half_cols].astype(F32)
+    grad_out = jnp.concatenate([halves[0] + halves[2], halves[1] + halves[3]], axis=1)
+    grad_up = up_all.transpose(1, 0, 2).astype(F32)
+    grad_down = down_all.transpose(2, 0, 1).astype(F32)
+    return (
+        block_out,
+        mean_loss,
+        input_grad,
+        own[GAIN_ONE],
+        own[BIAS_ONE],
+        grad_qkv,
+        grad_out,
+        own[GAIN_TWO],
+        own[BIAS_TWO],
+        own[:EXPERTS].T,
+        grad_up,
+        grad_down,
     )
 
 

time: 769 us -> 397 us (0.52)
  waiting for transfers between devices: 387 us -> 0 us
  Pallas kernels: 0 us -> 340 us
  matrix products: 125 us -> 0 us
  blocking collectives: 95.4 us -> 0 us
  local copies, waits for them, and re-layouts: 91.7 us -> 36.1 us
  other arithmetic: 30.7 us -> 10.1 us
  between operations: 18 us -> 3.46 us
  starting transfers between devices: 14 us -> 0 us
    pallas_call x0 -> x1, Pallas kernels: none -> 340 us  [run_block(): pl.pallas_call(lambda *refs: block_kernel(sizes, *refs), out_shape=(shape...]
    all_gather x6 -> x0, waiting for transfers between devices: 177 us -> none  [the longest x1 57.3 us: on_device(): lax.all_gather(lax.dynamic_index_in_dim(expert_out, seq_place, 1, keepdim...]
    reduce_scatter x4 -> x0, waiting for transfers between devices: 140 us -> none  [the longest x1 99.7 us: on_device(): lax.psum_scatter(grad_down, 'fsdp', scatter_dimension=0, tiled=True)]
    dot_general x25 -> x0, matrix products: 117 us -> none  [the longest x15 83.8 us: dot32(): lax.dot_general(left, right, (dims, ((), ())), preferred_element_type=F32)]
    all_to_all x3 -> x0, blocking collectives: 46.9 us -> none  [the longest x1 17.5 us: on_device(): lax.all_to_all(returned_grad, 'seq', split_axis=0, concat_axis=0, tiled=T...]
    unnamed x12 -> x0, waiting for transfers between devices: 41.2 us -> none
    psum x1 -> x0, blocking collectives: 38.2 us -> none  [on_device(): vectors = lax.psum(vectors, ('fsdp', 'seq'))]
    all_to_all x3 -> x0, waiting for transfers between devices: 28.6 us -> none  [the longest x1 11.1 us: on_device(): lax.all_to_all(dispatch_grad.reshape(pieces, capacity, features), 'seq',...]
  transfers between devices with their start and end apart: 14 -> 0, of which waited for: 13 -> 0; matrix products, arithmetic and copies ran while one was open for 23% -> 0% of each run, Pallas kernels for 0% -> 0%
where the time goes in v2:
time: 397 us; the launch traced here: 390 us
  Pallas kernels  340 us (86%)
  local copies, waits for them, and re-layouts  36.1 us (9%)
  other arithmetic  10.1 us (3%)
    pallas_call x1, Pallas kernels, run_block(): pl.pallas_call(lambda *refs: block_kernel(sizes, *refs), out_shape=(shape...  340 us
    unnamed x42, local copies, waits for them, and re-layouts  20.1 us

profile of v2, /device:TPU:25, one launch (start us, length us, event | category | flops | bytes accessed | tf_op | source)
XLA Modules:
  0.0 389.6 jit_solution(13493043780626114190)
XLA Ops:
  0.6 0.0 copy-start
  0.7 1.0 constant_dynamic-slice_fusion.3
  1.7 1.6 reshape.128
  3.4 0.3 constant_dynamic-slice_fusion.2
  3.7 0.2 copy.63
  3.9 0.2 copy.51
  4.1 0.7 pad_maximum_fusion.1.refs_5_
  4.8 0.0 copy-done.15
  4.8 0.6 fusion.4
  5.4 0.6 iota_compare_fusion.1
  6.1 0.1 broadcast_and_fusion
  6.1 0.1 and_convert_fusion
  6.3 0.1 reshape.127
  6.4 0.8 copy.56.refs_2_
  7.2 0.0 copy-done
  7.2 1.2 constant_dynamic-slice_fusion
  8.4 0.9 copy.69
  9.3 1.2 constant_dynamic-slice_fusion.1
  10.5 0.0 copy-done.7
  10.5 0.0 copy-start.4
  10.5 0.0 copy-start.10
  10.5 0.0 copy-start.11
  10.5 0.0 copy-start.12
  10.6 0.0 copy-start.13
  10.6 0.0 copy-start.14
  10.6 1.0 copy.70
  11.6 0.0 copy-done.3
  11.6 1.0 copy.54.refs_0_
  12.6 0.0 copy-done.4
  12.6 1.0 copy.55.refs_1_
  13.6 0.0 copy-done.10
  13.6 0.0 copy-done.12
  13.6 0.6 pad.9.refs_4_
  14.2 340.0 %block.1 = (f32[2,145,768]{2,1,0:T(8,128)}, f32[2,145,768]{2,1,0:T(8,128)}, f32[16,768]{1,0:T(8,128)}, bf16[4,96,960]{2,1,0:T(8,128)(2,1)}, bf16[4,96,3072]{2,1,...) custom-call(f32[2,145,768]{2,1,0:T(8,128)} %copy.54.refs_0_, ...), custom_call_target="tpu_custom_call" | custom-call | tf_op jit(solution)/shard_map/block/pallas_call | solution.py:901
  354.3 2.2 convert_bitcast_fusion.1
  356.5 5.2 %copy.61 = f32[96,4,3072]{2,1,0:T(4,128)} copy(f32[96,4,3072]{2,0,1:T(8,128)S(1)} %convert_bitcast_fusion.1) | data formatting | bytes 9437184
  361.7 2.4 convert_bitcast_fusion
  364.2 6.7 %copy.62 = f32[384,4,768]{2,1,0:T(4,128)} copy(f32[384,4,768]{0,2,1:T(8,128)} %convert_bitcast_fusion) | data formatting | bytes 9437184
  371.0 0.7 pad_maximum_fusion
  371.7 1.0 slice_convert_fusion
  372.8 1.6 copy.57
  374.3 1.5 copy.58
  375.9 3.0 reshape.130
  378.9 2.6 copy.59
  381.5 1.4 copy.60
  382.8 1.4 dynamic-slice_bitcast_fusion.1
  384.3 1.3 dynamic-slice_bitcast_fusion
  385.6 1.4 slice_reduce_fusion
  (26 shorter events, 0.2 us)
Async XLA Ops:
  0.6 6.5 %copy-start = (bf16[384,4,768]{2,1,0:T(4,128)(2,1)S(1)}, bf16[384,4,768]{2,1,0:T(4,128)(2,1)}, u32[]{:S(2)}) copy-start(bf16[384,4,768]{2,1,0:T(4,128)(2,1)} %param.27) | copy-start | bytes 7077892
  0.7 4.1 %copy-start.15 = (s32[8]{0:T(128)S(1)}, s32[8]{0:T(128)}, u32[]{:S(2)}) copy-start(s32[8]{0:T(128)} %param.16) | copy-start | bytes 100
  0.7 5.5 %copy-start.8 = (s32[1,2,145,2]{2,3,1,0:T(2,128)S(1)}, s32[1,2,145,2]{2,3,1,0:T(2,128)}, u32[]{:S(2)}) copy-start(s32[1,2,145,2]{2,3,1,0:T(2,128)} %param.18) | copy-start | bytes 6964
  0.7 5.5 %copy-start.9 = (s32[1,2,145,2]{2,3,1,0:T(2,128)S(1)}, s32[1,2,145,2]{2,3,1,0:T(2,128)}, u32[]{:S(2)}) copy-start(s32[1,2,145,2]{2,3,1,0:T(2,128)} %param.17) | copy-start | bytes 6964
  6.4 4.1 %copy-start.7 = (s32[320,8]{0,1:T(8,128)}, s32[320,8]{0,1:T(8,128)S(1)}, u32[]{:S(2)}) copy-start(s32[320,8]{0,1:T(8,128)S(1)} %reshape.127) | copy-start | bytes 30724
  7.2 2.1 copy-start.6
  9.3 2.3 copy-start.3
  10.5 2.1 copy-start.4
  10.5 3.0 copy-start.10
  10.5 3.0 copy-start.11
  10.5 3.0 copy-start.12
  10.6 3.0 copy-start.13
  10.6 3.0 copy-start.14
  356.5 5.2 %copy-start.1 = (bf16[4,768,384]{2,1,0:T(8,128)(2,1)S(1)}, bf16[4,768,384]{2,1,0:T(8,128)(2,1)}, u32[]{:S(2)}) copy-start(bf16[4,768,384]{2,1,0:T(8,128)(2,1)} %get-tuple-element.23) | copy-start | bytes 7077892
  364.2 6.8 %copy-start.5 = (bf16[4,96,960]{2,1,0:T(8,128)(2,1)S(1)}, bf16[4,96,960]{2,1,0:T(8,128)(2,1)}, u32[]{:S(2)}) copy-start(bf16[4,96,960]{2,1,0:T(8,128)(2,1)} %get-tuple-element.21) | copy-start | bytes 2211844
  375.9 5.6 %copy-start.2 = (f32[2,145,768]{2,1,0:T(8,128)S(1)}, f32[2,145,768]{2,1,0:T(8,128)}, u32[]{:S(2)}) copy-start(f32[2,145,768]{2,1,0:T(8,128)} %get-tuple-element.50) | copy-start | bytes 2672644
